TPU v7x, 128 devices: a whole 4x4x4 slice. The times are simulated.
128 devices in a mesh: tm: 32 (over y, x, core), sensor: 4 (over z).
Axes of the slice: x: 4, y: 4, z: 4, core: 2. Of those that a mesh axis runs over, the one named last changes fastest.
Arguments:
- observation_operator: bfloat16 [32768, 128, 128], P(('tm', 'sensor')), may hold values from -0.1875 to 0.1875
- observed_values: bfloat16 [32768, 128], P(('tm', 'sensor')), may hold values from -6 to 6
- observation_weight: float32 [32768, 128], P(('tm', 'sensor')), may hold values from 0.1 to 1
- tile_time_step: int32 [32768], P(('tm', 'sensor')), may hold values from 0 to 127
- tile_state_block: int32 [32768], P(('tm', 'sensor')), may hold values from 0 to 3
- tile_live_count: int32 [32768], P(('tm', 'sensor')), may hold values from 1 to 128
- transition: float32 [512, 512], replicated, may hold values from -1 to 1, as said below
- predicted_precision: float32 [512], replicated, may hold values from 1 to 1000
- starting_mean: float32 [512], replicated, may hold values from -6 to 6
Outputs:
- filtered: float32 [128, 512], P('tm')
- smoothed: float32 [128, 512], P('tm')
Inputs may be any that keep to these rules, and one draw needn't show every extreme that they name: `transition`: a dense real matrix.
All inputs are finite; a program needn't handle non-finite values.
Results may differ from a plain program's by a relative error of at most 0.0045.
Values sent between devices are 32-bit elements; how exact they have to be, the bound alone decides.
A program may use at most 128 MiB of HBM per device.

v0:
```python
import jax
import jax.numpy as jnp
from jax import lax
from jax.sharding import PartitionSpec as P

STEPS_DEV = 4


top_precision = lax.Precision.HIGHEST


def prefix(shard, axis, combine, identity, reverse):
    peers, index = (lax.axis_size(axis), lax.axis_index(axis))
    everything = jax.tree.map(lambda part: lax.all_gather(part, axis), shard)
    start = jax.tree.map(
        lambda part, zero: jnp.broadcast_to(jnp.asarray(zero, part.dtype), part.shape),
        shard,
        identity,
    )

    def hop(k, before):
        at = peers - 1 - k if reverse else k
        reached = at > index if reverse else at < index
        new = combine(before, jax.tree.map(lambda part: part[at], everything))
        return jax.tree.map(lambda a, b: jnp.where(reached, a, b), new, before)

    return lax.fori_loop(0, peers, hop, start)


def compose_maps(earlier, later):
    return (
        jnp.dot(later[0], earlier[0], precision=top_precision),
        jnp.dot(later[0], earlier[1], precision=top_precision) + later[1],
    )


def shards(
    observation_operator,
    observed_values,
    observation_weight,
    tile_time_step,
    tile_state_block,
    tile_live_count,
    transition,
    predicted_precision,
    starting_mean,
):
    tile_total = observation_operator.shape[0]
    tile_rows = observation_operator.shape[1]
    width = transition.shape[0]
    block_count = width // tile_rows
    time_size = lax.axis_size("tm")
    step_count = STEPS_DEV
    position = lax.axis_index("tm")
    columns = lax.broadcasted_iota(jnp.int32, (tile_total, tile_rows), 1)
    live_weight = jnp.where(columns < tile_live_count[:, None], observation_weight, 0.0)
    weighted = (live_weight * observed_values.astype(jnp.float32)).astype(jnp.bfloat16)
    tile_info = jnp.einsum(
        "tko,tk->to", observation_operator, weighted, preferred_element_type=jnp.float32
    )
    squared = jnp.square(observation_operator.astype(jnp.float32))
    tile_curv = jnp.sum(squared * live_weight[:, :, None], axis=1)
    stacked = jnp.concatenate([tile_info, tile_curv], axis=1)
    upper_part = stacked.astype(jnp.bfloat16)
    remainder = stacked - upper_part.astype(jnp.float32)
    middle_part = remainder.astype(jnp.bfloat16)
    lower_part = (remainder - middle_part.astype(jnp.float32)).astype(jnp.bfloat16)
    split_stack = jnp.concatenate([upper_part, middle_part, lower_part], axis=1)
    stack_width = stacked.shape[1]
    segment_ids = tile_time_step * block_count + tile_state_block
    targets = lax.broadcasted_iota(
        jnp.int32, (step_count * lax.axis_size("tm") * block_count, tile_total), 0
    )
    onehot = (targets == segment_ids[None, :]).astype(jnp.bfloat16)
    pieces = jnp.dot(onehot, split_stack, preferred_element_type=jnp.float32)
    summed = (
        pieces[:, :stack_width]
        + pieces[:, stack_width : 2 * stack_width]
        + pieces[:, 2 * stack_width :]
    )
    summed = summed.reshape(step_count * lax.axis_size("tm"), block_count, 2, tile_rows).transpose(
        0, 2, 1, 3
    )
    gathered = lax.psum_scatter(
        summed.reshape(step_count * lax.axis_size("tm"), 2 * width),
        "tm",
        scatter_dimension=0,
        tiled=True,
    )
    gathered = lax.psum(gathered, "sensor")
    information = gathered[:, :width]
    observed_flag = gathered[:, width:]
    precision_row_list = predicted_precision[None, :] + observed_flag
    kalman_gain_rows = predicted_precision[None, :] / precision_row_list
    drive_rows = information / precision_row_list
    final_row = (position == time_size - 1) & (
        lax.broadcasted_iota(jnp.int32, (step_count, 1), 0) == step_count - 1
    )
    smooth_gain = jnp.where(final_row, 0.0, kalman_gain_rows)
    transposed = transition.T
    identity = jnp.eye(width, dtype=jnp.float32)
    zero_vec = jnp.zeros((width,), jnp.float32)

    def compose_forward(state_pair, inputs):
        gain_row, drive_row = inputs
        matrix_part = gain_row[:, None] * jnp.dot(
            transition, state_pair[0], precision=top_precision
        )
        vector_part = (
            gain_row * jnp.dot(transition, state_pair[1], precision=top_precision) + drive_row
        )
        return ((matrix_part, vector_part), None)

    forward_map, _ = lax.scan(compose_forward, (identity, zero_vec), (kalman_gain_rows, drive_rows))
    prior_map = prefix(forward_map, "tm", compose_maps, (identity, zero_vec), False)
    entry_vec = jnp.dot(prior_map[0], starting_mean, precision=top_precision) + prior_map[1]

    def advance(mean_vec, inputs):
        gain_row, drive_row = inputs
        mean_vec = gain_row * jnp.dot(transition, mean_vec, precision=top_precision) + drive_row
        return (mean_vec, mean_vec)

    _, filtered = lax.scan(advance, entry_vec, (kalman_gain_rows, drive_rows))
    pushed = jnp.dot(
        jnp.dot(filtered, transposed, precision=top_precision), transition, precision=top_precision
    )
    offsets = filtered - smooth_gain * pushed

    def compose_backward(state_pair, inputs):
        gain_row, offset_row = inputs
        matrix_part = gain_row[:, None] * jnp.dot(
            transposed, state_pair[0], precision=top_precision
        )
        vector_part = (
            gain_row * jnp.dot(transposed, state_pair[1], precision=top_precision) + offset_row
        )
        return ((matrix_part, vector_part), None)

    backward_map, _ = lax.scan(
        compose_backward, (identity, zero_vec), (smooth_gain, offsets), reverse=True
    )
    after_map = prefix(backward_map, "tm", compose_maps, (identity, zero_vec), True)
    exit_vec = after_map[1]

    def retreat(later_vec, inputs):
        gain_row, offset_row = inputs
        value = gain_row * jnp.dot(transposed, later_vec, precision=top_precision) + offset_row
        return (value, value)

    _, smoothed = lax.scan(retreat, exit_vec, (smooth_gain, offsets), reverse=True)
    return (filtered, smoothed)


def solution(mesh):
    in_specs = (
        P(("tm", "sensor"), None, None),
        P(("tm", "sensor"), None),
        P(("tm", "sensor"), None),
        P(("tm", "sensor")),
        P(("tm", "sensor")),
        P(("tm", "sensor")),
        P(),
        P(),
        P(),
    )
    out_specs = (P("tm", None), P("tm", None))
    return jax.shard_map(shards, mesh=mesh, in_specs=in_specs, out_specs=out_specs, check_vma=False)
```

profile of v0, /device:TPU:1, one launch (start us, length us, event | category | flops | bytes accessed | tf_op | source)
XLA Modules:
  0.0 735.2 jit_solution(15980185921461645022)
XLA Ops:
  8.4 5.6 fusion.22
  14.0 8.3 %multiply_reduce_fusion = f32[256,128]{1,0:T(8,128)S(1)} fusion(bf16[256,128,128]{2,1,0:T(8,128)(2,1)} %param.21, f32[256,128]{1,0:T(8,128)S(1)} %get-tuple-element.717), kind=kLoop, calls=%fused_computation.34 | loop fusion | flops 16744448 | bytes 8650752 | tf_op jit(solution)/shard_map/reduce_sum | solution.py:62
  25.9 105.1 %all-reduce.3.cloned.1.call-done = f32[128,1024]{1,0:T(8,128)} async-done(((f32[128,1024]{1,0:T(8,128)}), f32[128,1024]{1,0:T(8,128)}) %all-reduce.3.cloned.1.call-update) | async-done | bytes 524304
  131.8 13.3 %psum.7 = f32[4,1024]{1,0:T(4,128)S(1)} all-reduce(f32[4,1024]{1,0:T(4,128)S(1)} %constant_dynamic-slice_fusion.10), channel_id=1, replica_groups=mesh['tm'=32,'sensor'=4] {'sensor'}, use_global_device_ids=true, to_apply=%region_2.3 | all-reduce | flops 4096 | bytes 32768 | tf_op jit(solution)/shard_map/psum | solution.py:90
  145.2 11.9 %while.92 = (s32[]{:T(128)}, f32[512,512]{1,0:T(8,128)S(1)}, f32[512]{0:T(512)S(1)}, f32[4,512]{1,0:T(4,128)S(1)}, f32[512,512]{1,0:T(8,128)S(1)}, /*index=5*/f32[4,512]{1,0:T(4,128)S(1)}, s32[]{:T(128)}, s32[]{:T(128)}) while((s32[]{:T(128)}, f32[512,512]{1,0:T(8,128)S(1)}, f32[512]{0:T(512)S(1)}, f32[4,512]{1,0:T(4,128)S(1)}, ...), condition=%wide.region_4.5_spmd.clone, body=%wide.region_3.4_spmd.clone.sunk | while | flops 1614022144 | bytes 6318179 | solution.py:114
  159.5 29.1 %all-gather.4 = f32[32,1,512]{2,1,0:T(1,128)S(1)} all-gather(f32[1,1,512]{2,1,0:T(1,128)S(1)} %bitcast.193), channel_id=3, replica_groups=mesh['tm'=32,'sensor'=4] {'tm'}, dimensions={0}, use_global_device_ids=true | all-gather | bytes 67584 | tf_op jit(solution)/shard_map/all_gather | solution.py:14
  188.7 84.7 %all-gather.9.cloned.1.call-done = f32[16384,512]{1,0:T(8,128)} async-done(((f32[512,512]{1,0:T(8,128)}), f32[16384,512]{1,0:T(8,128)}) %all-gather.9.cloned.1.call-update) | async-done | bytes 33554448 | tf_op jit(solution)/shard_map/all_gather | solution.py:14
  273.3 242.8 %while.93 = (s32[]{:T(128)}, f32[512,512]{1,0:T(8,128)}, f32[512]{0:T(512)S(1)}, s32[]{:T(128)}, f32[32,512,512]{2,1,0:T(8,128)}, /*index=5*/f32[32,512]{1,0:T(8,128)S(1)}, s32[]{:T(128)}, s32[]{:T(128)}) while((s32[]{:T(128)}, f32[512,512]{1,0:T(8,128)}, f32[512]{0:T(512)S(1)}, s32[]{:T(128)}, f32[32,512,512]{2,1,0:T(8,128)}, ...), condition=%wide.region_6.7_spmd.clone, body=%wide.region_5.6_spmd.clone.sunk | while | flops 1614022656 | bytes 7361647 | solution.py:27
  276.8 4.1 convolution_select_fusion.2
  284.4 4.1 convolution_select_fusion.2
  292.0 4.1 convolution_select_fusion.2
  299.6 4.1 convolution_select_fusion.2
  307.2 4.1 convolution_select_fusion.2
  314.8 4.1 convolution_select_fusion.2
  322.3 4.1 convolution_select_fusion.2
  329.9 4.1 convolution_select_fusion.2
  337.5 4.1 convolution_select_fusion.2
  345.1 4.1 convolution_select_fusion.2
  352.7 4.1 convolution_select_fusion.2
  360.3 4.1 convolution_select_fusion.2
  367.9 4.1 convolution_select_fusion.2
  375.5 4.1 convolution_select_fusion.2
  383.0 4.1 convolution_select_fusion.2
  390.6 4.1 convolution_select_fusion.2
  398.2 4.1 convolution_select_fusion.2
  405.8 4.1 convolution_select_fusion.2
  413.4 4.1 convolution_select_fusion.2
  421.0 4.1 convolution_select_fusion.2
  428.6 4.1 convolution_select_fusion.2
  436.2 4.1 convolution_select_fusion.2
  443.7 4.1 convolution_select_fusion.2
  451.3 4.1 convolution_select_fusion.2
  458.9 4.1 convolution_select_fusion.2
  466.5 4.1 convolution_select_fusion.2
  474.1 4.1 convolution_select_fusion.2
  481.7 4.1 convolution_select_fusion.2
  489.3 4.1 convolution_select_fusion.2
  496.8 4.1 convolution_select_fusion.2
  504.4 4.1 convolution_select_fusion.2
  512.0 4.1 convolution_select_fusion.2
  518.4 4.3 while.90
  524.3 12.0 %while.94 = (s32[]{:T(128)}, f32[512,512]{1,0:T(8,128)S(1)}, f32[512]{0:T(512)S(1)}, f32[4,512]{1,0:T(4,128)S(1)}, f32[512,512]{1,0:T(8,128)S(1)}, /*index=5*/f3...) while((s32[]{:T(128)}, f32[512,512]{1,0:T(8,128)S(1)}, f32[512]{0:T(512)S(1)}, ...), condition=%wide.region_10.11_spmd.clone, body=%wide.region_9.10_spmd.clone.sunk | while | flops 1614022144 | bytes 6318199 | solution.py:139
  537.3 23.9 %all-gather.5 = f32[32,1,512]{2,1,0:T(1,128)S(1)} all-gather(f32[1,1,512]{2,1,0:T(1,128)S(1)} %bitcast.192), channel_id=5, replica_groups=mesh['tm'=32,'sensor'=4] {'tm'}, dimensions={0}, use_global_device_ids=true | all-gather | bytes 67584 | tf_op jit(solution)/shard_map/all_gather | solution.py:14
  561.2 89.4 %all-gather.11.cloned.1.call-done = f32[16384,512]{1,0:T(8,128)} async-done(((f32[512,512]{1,0:T(8,128)}), f32[16384,512]{1,0:T(8,128)}) %all-gather.11.cloned.1.call-update) | async-done | bytes 33554448 | tf_op jit(solution)/shard_map/all_gather | solution.py:14
  650.6 73.2 %while.95 = (s32[]{:T(128)}, f32[512]{0:T(512)S(1)}, s32[]{:T(128)}, f32[32,512,512]{2,1,0:T(8,128)}, f32[32,512]{1,0:T(8,128)S(1)}, /*index=5*/s32[]{:T(128)}, s32[]{:T(128)}, s32[]{:T(128)}, s32[]{:T(128)}) while((s32[]{:T(128)}, f32[512]{0:T(512)S(1)}, s32[]{:T(128)}, f32[32,512,512]{2,1,0:T(8,128)}, ...), condition=%wide.region_12.13_spmd.clone, body=%wide.region_11.12_spmd.clone.sunk | while | flops 3147784 | bytes 1069224 | solution.py:27
  655.1 2.2 fusion.105
  657.4 2.2 fusion.105
  659.7 2.2 fusion.105
  662.0 2.2 fusion.105
  664.3 2.2 fusion.105
  666.6 2.2 fusion.105
  668.9 2.2 fusion.105
  671.2 2.2 fusion.105
  673.4 2.2 fusion.105
  675.7 2.2 fusion.105
  678.0 2.2 fusion.105
  680.3 2.2 fusion.105
  682.6 2.2 fusion.105
  684.9 2.2 fusion.105
  689.5 2.2 fusion.105
  691.7 2.2 fusion.105
  694.0 2.2 fusion.105
  698.6 2.2 fusion.105
  723.8 4.3 while.91
  (405 shorter events, 187.1 us)
Async XLA Ops:
  7.2 509.0 %copy-start = (f32[512]{0:T(512)S(1)}, f32[512]{0:T(512)}, u32[]{:S(2)}) copy-start(f32[512]{0:T(512)} %param.29) | copy-start | bytes 6148
  7.2 17.5 %copy-start.9 = (u32[128]{0:T(128)S(1)}, u32[128]{0:T(128)}, u32[]{:S(2)}) copy-start(u32[128]{0:T(128)} %constant.172) | copy-start | bytes 1540
  7.2 15.2 %copy-start.8 = (s32[256]{0:T(256)S(1)}, s32[256]{0:T(256)}, u32[]{:S(2)}) copy-start(s32[256]{0:T(256)} %param.24) | copy-start | bytes 3076
  7.2 15.2 %copy-start.7 = (s32[256]{0:T(256)S(1)}, s32[256]{0:T(256)}, u32[]{:S(2)}) copy-start(s32[256]{0:T(256)} %param.25) | copy-start | bytes 3076
  7.2 137.9 %copy-start.6 = (f32[512]{0:T(512)S(1)}, f32[512]{0:T(512)}, u32[]{:S(2)}) copy-start(f32[512]{0:T(512)} %param.28) | copy-start | bytes 6148
  7.2 137.9 %copy-start.1 = (f32[512,512]{1,0:T(8,128)S(1)}, f32[512,512]{1,0:T(8,128)}, u32[]{:S(2)}) copy-start(f32[512,512]{1,0:T(8,128)} %param.27) | copy-start | bytes 3145732
  7.2 123.8 %all-reduce.3.cloned.1.call-start = ((), (), s32[]{:S(2)}) async-start(), calls=%async_computation.2 | async-start | bytes 1048576
  24.4 249.0 %all-gather.9.cloned.1.call-start = ((), (), s32[]{:S(2)}) async-start(), calls=%async_computation | async-start | bytes 34603008 | tf_op jit(solution)/shard_map/all_gather | solution.py:14
  157.1 1.0 copy-start.3
  158.1 492.5 %all-gather.11.cloned.1.call-start = ((), (), s32[]{:S(2)}) async-start(), calls=%async_computation.1 | async-start | bytes 34603008 | tf_op jit(solution)/shard_map/all_gather | solution.py:14
  522.7 1.6 copy-start.4
  536.2 1.0 copy-start.2
  728.1 0.6 copy-start.5
Sparse Core Ops, SparseCore 0:
  24.5 106.4 all-reduce.2
  158.2 115.0 all-gather.8
  537.4 113.1 all-gather.10
where the time goes:
time: 741 us; the launch traced here: 735 us
  matrix products  313 us (42%)
  waiting for transfers between devices  279 us (38%)
  blocking collectives  66.3 us (9%)
  local copies, waits for them, and re-layouts  48.4 us (7%)
  between operations  14.7 us (2%)
  other arithmetic  11 us (1%)
    all_gather x2, waiting for transfers between devices, prefix(): everything = jax.tree.map(lambda part: lax.all_gather(part, axis), shard)  174 us
    dot_general x64, matrix products, compose_maps(): jnp.dot(later[0], earlier[1], precision=top_precision) + later[1]  141 us
    dot_general x32, matrix products, compose_maps(): jnp.dot(later[0], earlier[0], precision=top_precision)  132 us
    unnamed x4, waiting for transfers between devices  105 us
    all_gather x2, blocking collectives, prefix(): everything = jax.tree.map(lambda part: lax.all_gather(part, axis), shard)  53 us
    while x40, local copies, waits for them, and re-layouts  39.9 us
  transfers between devices with their start and end apart: 3, of which 3 were waited for; matrix products, arithmetic and copies ran while one was open for 0% of the time, Pallas kernels for 0%

commit v1 on v0

v1 whole, which is shorter than its diff:
```python
import functools

import jax
import jax.numpy as jnp
from jax import lax
from jax.experimental import pallas as pl
from jax.experimental.pallas import tpu as pltpu
from jax.sharding import PartitionSpec as P

MESH = pl.DeviceIdType.MESH
TILE = 128
GROUPS = (("c",), ("x", "y", "z"))
SIZES = {"c": 2, "x": 4, "y": 4, "z": 4}
F32, BF16 = jnp.float32, jnp.bfloat16


def parts(value):
    upper = value.astype(BF16)
    return upper, (value - upper.astype(F32)).astype(BF16)


def tile_kernel(steps, op_ref, val_ref, wgt_ref, step_ref, block_ref, live_ref, out_ref, lhs, info, curv):
    k = pl.program_id(0)
    tiles = wgt_ref.shape[0]

    @pl.when(k == 0)
    def _():
        for half in range(tiles // TILE):
            rows = pl.ds(half * TILE, TILE)
            count = live_ref[:, half * TILE : (half + 1) * TILE].astype(F32)
            count = jnp.transpose(jnp.broadcast_to(count, (TILE, TILE)))
            columns = lax.broadcasted_iota(jnp.int32, (TILE, TILE), 1).astype(F32)
            live = jnp.where(columns < count, wgt_ref[rows, :], 0.0)
            weighted = (live * val_ref[rows, :].astype(F32)).astype(BF16).astype(F32)
            upper = live.astype(BF16).astype(F32)
            lower = live - upper
            for kind, value in enumerate((weighted, upper, lower, jnp.zeros_like(live))):
                lhs[pl.ds(half * TILE // 8, TILE // 8), kind * 8 : (kind + 1) * 8, :] = value.reshape(
                    TILE // 8, 8, TILE
                )

    each = op_ref.shape[0]
    place = lax.broadcasted_iota(jnp.int32, (8, TILE), 0)
    for group in range(each // 8):
        left = lhs[k * (each // 8) + group].astype(BF16)
        info_sum = jnp.zeros((8, TILE), F32)
        curv_sum = jnp.zeros((8, TILE), F32)
        for j in range(8):
            op = op_ref[group * 8 + j]
            both = jnp.concatenate([op, op * op], axis=1)
            got = jnp.dot(left, both, preferred_element_type=F32)
            info_sum = jnp.where(place == j, got[0:8, :TILE], info_sum)
            curv_sum = jnp.where(place == j, got[8:16, TILE:] + got[16:24, TILE:], curv_sum)
        at = pl.ds(pl.multiple_of(k * each + group * 8, 8), 8)
        info[at, :] = info_sum
        curv[at, :] = curv_sum

    @pl.when(k == steps - 1)
    def _():
        segments = out_ref.shape[0] // 2
        ids = step_ref[...] * 4 + block_ref[...]
        targets = lax.broadcasted_iota(jnp.int32, (segments, tiles), 0)
        onehot = jnp.where(targets == ids, 1.0, 0.0).astype(BF16)
        stack = jnp.concatenate(parts(info[...]) + parts(curv[...]), axis=1)
        sums = jnp.dot(onehot, stack, preferred_element_type=F32)
        out_ref[:segments, :] = sums[:, :TILE] + sums[:, TILE : 2 * TILE]
        out_ref[segments:, :] = sums[:, 2 * TILE : 3 * TILE] + sums[:, 3 * TILE :]


def tile_sums(op, val, wgt, step, block, live, segments):
    tiles = op.shape[0]
    steps = 8
    each = tiles // steps

    def whole(*shape):
        return pl.BlockSpec(shape, lambda k: (0,) * len(shape))

    return pl.pallas_call(
        functools.partial(tile_kernel, steps),
        grid=(steps,),
        out_shape=jax.ShapeDtypeStruct((2 * segments, TILE), F32),
        in_specs=[
            pl.BlockSpec((each, TILE, TILE), lambda k: (k, 0, 0)),
            whole(tiles, TILE),
            whole(tiles, TILE),
            whole(1, tiles),
            whole(1, tiles),
            whole(1, tiles),
        ],
        out_specs=whole(2 * segments, TILE),
        scratch_shapes=[
            pltpu.VMEM((tiles // 8, 32, TILE), F32),
            pltpu.VMEM((tiles, TILE), F32),
            pltpu.VMEM((tiles, TILE), F32),
        ],
        compiler_params=pltpu.CompilerParams(vmem_limit_bytes=32 << 20),
    )(op, val, wgt, step.reshape(1, -1), block.reshape(1, -1), live.reshape(1, -1))


def exchange_kernel(in_ref, out_ref, *scratch):
    count = len(GROUPS)
    works, boxes = scratch[:count], scratch[count : 2 * count]
    send_in, recv_in, send_out, recv_out = scratch[2 * count :]
    tm = lax.axis_index("tm")
    mine = {
        "c": lax.rem(tm, 2),
        "x": lax.rem(lax.div(tm, 2), 4),
        "y": lax.div(tm, 8),
        "z": lax.axis_index("sensor"),
    }

    def device_of(at):
        return (at["y"] * 8 + at["x"] * 2 + at["c"], at["z"])

    def member(group, offset):
        at = dict(mine)
        for axis in group:
            at[axis] = lax.rem(mine[axis] + lax.rem(offset, SIZES[axis]), SIZES[axis])
            offset = lax.div(offset, SIZES[axis])
        return at

    def index_in(group, at):
        index, scale = 0, 1
        for axis in group:
            index = index + at[axis] * scale
            scale *= SIZES[axis]
        return index, scale

    barrier = pltpu.get_barrier_semaphore()
    greeted = 0
    for group in GROUPS:
        size = index_in(group, mine)[1]

        def greet(offset, carry, group=group):
            pl.semaphore_signal(
                barrier, inc=1, device_id=device_of(member(group, offset)), device_id_type=MESH
            )
            return carry

        lax.fori_loop(1, size, greet, 0)
        greeted += size - 1
    pl.semaphore_wait(barrier, greeted)

    source = in_ref
    start, starts = 0, []
    for stage, group in enumerate(GROUPS):
        me, size = index_in(group, mine)
        rows = source.shape[0] // size
        box = boxes[stage]

        def give(offset, carry, source=source, group=group, rows=rows, box=box, stage=stage):
            to = member(group, offset)
            index, _ = index_in(group, to)
            pltpu.make_async_remote_copy(
                src_ref=source.at[pl.ds(pl.multiple_of(index * rows, 8), rows)],
                dst_ref=box.at[pl.ds(pl.multiple_of((offset - 1) * rows, 8), rows)],
                send_sem=send_in.at[stage],
                recv_sem=recv_in.at[stage],
                device_id=device_of(to),
                device_id_type=MESH,
            ).start()
            return carry

        lax.fori_loop(1, size, give, 0)
        pltpu.make_async_copy(box, box, recv_in.at[stage]).wait()
        own = source[pl.ds(pl.multiple_of(me * rows, 8), rows), :]
        works[stage][...] = own + jnp.sum(box[...].reshape(size - 1, rows, TILE), axis=0)
        start = start + me * rows
        starts.append(start)
        source = works[stage]

    last = source.shape[0]
    out_ref[pl.ds(pl.multiple_of(start, 8), last), :] = source[...]
    for stage in reversed(range(count)):
        group = GROUPS[stage]
        size = index_in(group, mine)[1]
        rows = works[stage].shape[0]
        piece = out_ref.at[pl.ds(pl.multiple_of(starts[stage], 8), rows)]

        def spread(offset, carry, group=group, piece=piece, stage=stage):
            pltpu.make_async_remote_copy(
                src_ref=piece,
                dst_ref=piece,
                send_sem=send_out.at[stage],
                recv_sem=recv_out.at[stage],
                device_id=device_of(member(group, offset)),
                device_id_type=MESH,
            ).start()
            return carry

        lax.fori_loop(1, size, spread, 0)
        pltpu.make_async_copy(boxes[stage], boxes[stage], recv_out.at[stage]).wait()
    for stage in range(count):
        pltpu.make_async_copy(boxes[stage], boxes[stage], send_in.at[stage]).wait()
        pltpu.make_async_copy(boxes[stage], boxes[stage], send_out.at[stage]).wait()


def exchange(sums):
    rows, works, boxes = sums.shape[0], [], []
    for group in GROUPS:
        size = 1
        for axis in group:
            size *= SIZES[axis]
        rows //= size
        works.append(pltpu.VMEM((rows, TILE), F32))
        boxes.append(pltpu.VMEM(((size - 1) * rows, TILE), F32))
    return pl.pallas_call(
        exchange_kernel,
        out_shape=jax.ShapeDtypeStruct(sums.shape, F32),
        in_specs=[pl.BlockSpec(memory_space=pltpu.VMEM)],
        out_specs=pl.BlockSpec(memory_space=pltpu.VMEM),
        scratch_shapes=works + boxes + [pltpu.SemaphoreType.DMA((len(GROUPS),))] * 4,
        compiler_params=pltpu.CompilerParams(
            collective_id=0, has_side_effects=True, vmem_limit_bytes=16 << 20
        ),
    )(sums)


def recurrence_kernel(
    sums_ref, tran_ref, flip_ref, prec_ref, start_ref, filt_ref, smooth_ref,
    gain, drive, split, gain_col, diff_col, diff_row, filt_col, extra_row, extra_col, filt_row,
):
    segments = sums_ref.shape[0] // 2
    times = segments // 4
    width = tran_ref.shape[0]
    first = lax.axis_index("tm") * 2

    pp = prec_ref[...]
    pp = jnp.concatenate([pp, pp], axis=0)[None]
    observed = sums_ref[segments:, :].reshape(segments // 8, 8, TILE)
    precision = pp + observed
    inverse = 1.0 / precision
    gain[...] = (pp * inverse).reshape(segments, TILE)
    drive[...] = (sums_ref[:segments, :].reshape(segments // 8, 8, TILE) * inverse).reshape(segments, TILE)
    for kind, ref in enumerate((gain, drive)):
        for b in range(4):
            turned = jnp.transpose(ref[pl.ds(b, times, 4), :])
            upper, lower = parts(turned)
            rows = pl.ds(kind * width + b * TILE, TILE)
            split[rows, :TILE] = upper
            split[rows, TILE:] = lower

    lanes = lax.rem(lax.broadcasted_iota(jnp.int32, (2 * TILE, TILE), 0), TILE)

    def row_to_col(ref, row):
        total = ref[:, :TILE] * row[0]
        for b in range(1, 4):
            total += ref[:, b * TILE : (b + 1) * TILE] * row[b]
        return jnp.sum(total, axis=1, keepdims=True)

    def col_to_row(ref, col):
        return tuple(
            jnp.sum(ref[:, b * TILE : (b + 1) * TILE] * col, axis=0, keepdims=True) for b in range(4)
        )

    def forward(keep, i, row):
        even, odd = 2 * i, 2 * i + 1
        pick = jnp.where(lanes == even, 1.0, 0.0).astype(BF16)
        spread = jnp.dot(split[...], pick, preferred_element_type=F32)
        g_col = spread[:width]
        pushed = row_to_col(tran_ref, row)
        col = g_col * pushed + spread[width:]
        gain_col[i] = g_col
        diff_col[i] = col - pushed
        moved = col_to_row(flip_ref, col)
        out = []
        for b in range(4):
            at = pl.ds(4 * odd + b, 1)
            value = gain[at, :] * moved[b] + drive[at, :]
            diff_row[at, :] = value - moved[b]
            out.append(value)
            if keep is not None:
                filt_row[pl.ds(keep * 4 + b, 1), :] = value
        if keep is not None:
            filt_col[keep] = col
        return tuple(out)

    row = tuple(start_ref[b : b + 1, :] for b in range(4))
    plain = functools.partial(forward, None)
    row = lax.fori_loop(0, first, plain, row)
    row = forward(0, first, row)
    row = forward(1, first + 1, row)
    row = lax.fori_loop(first + 2, times // 2, plain, row)

    ahead = -jnp.broadcast_to(row_to_col(tran_ref, row), (width, TILE))
    gain[4 * (times - 1) :, :] = jnp.zeros((4, TILE), F32)

    def backward(keep, n, ahead):
        i = times // 2 - 1 - n
        odd = 2 * i + 1
        moved = col_to_row(tran_ref, ahead)
        back = []
        for b in range(4):
            at = pl.ds(4 * odd + b, 1)
            value = gain[at, :] * moved[b]
            back.append(value + diff_row[at, :])
            if keep is not None:
                extra_row[pl.ds(keep * 4 + b, 1), :] = value
        col = gain_col[i] * row_to_col(flip_ref, back)
        if keep is not None:
            extra_col[keep] = col
        return col + diff_col[i]

    plain = functools.partial(backward, None)
    half = times // 2
    ahead = lax.fori_loop(0, half - 2 - first, plain, ahead)
    ahead = backward(1, half - 2 - first, ahead)
    ahead = backward(0, half - 1 - first, ahead)
    lax.fori_loop(half - first, half, plain, ahead)

    eye = lax.broadcasted_iota(jnp.int32, (TILE, TILE), 0) == lax.broadcasted_iota(jnp.int32, (TILE, TILE), 1)
    for keep in range(2):
        for b in range(4):
            rows, lane = slice(b * TILE, (b + 1) * TILE), slice(b * TILE, (b + 1) * TILE)
            f = jnp.sum(jnp.where(eye, filt_col[keep, rows, :], 0.0), axis=0, keepdims=True)
            e = jnp.sum(jnp.where(eye, extra_col[keep, rows, :], 0.0), axis=0, keepdims=True)
            filt_ref[2 * keep : 2 * keep + 1, lane] = f
            smooth_ref[2 * keep : 2 * keep + 1, lane] = f + e
            f = filt_row[keep * 4 + b : keep * 4 + b + 1, :]
            filt_ref[2 * keep + 1 : 2 * keep + 2, lane] = f
            smooth_ref[2 * keep + 1 : 2 * keep + 2, lane] = f + extra_row[keep * 4 + b : keep * 4 + b + 1, :]


def recurrence(sums, transition, predicted_precision, starting_mean):
    segments = sums.shape[0] // 2
    width = transition.shape[0]
    times = segments // 4
    vmem = pl.BlockSpec(memory_space=pltpu.VMEM)
    shape = jax.ShapeDtypeStruct((4, width), F32)
    return pl.pallas_call(
        recurrence_kernel,
        out_shape=(shape, shape),
        in_specs=[vmem] * 5,
        out_specs=(vmem, vmem),
        scratch_shapes=[
            pltpu.VMEM((segments, TILE), F32),
            pltpu.VMEM((segments, TILE), F32),
            pltpu.VMEM((2 * width, 2 * TILE), BF16),
            pltpu.VMEM((times // 2, width, TILE), F32),
            pltpu.VMEM((times // 2, width, TILE), F32),
            pltpu.VMEM((segments, TILE), F32),
            pltpu.VMEM((2, width, TILE), F32),
            pltpu.VMEM((8, TILE), F32),
            pltpu.VMEM((2, width, TILE), F32),
            pltpu.VMEM((8, TILE), F32),
        ],
        compiler_params=pltpu.CompilerParams(vmem_limit_bytes=48 << 20),
    )(
        sums,
        transition,
        transition.T,
        predicted_precision.reshape(4, TILE),
        starting_mean.reshape(4, TILE),
    )


def shards(op, val, wgt, step, block, live, transition, predicted_precision, starting_mean):
    segments = 4 * 4 * lax.axis_size("tm")
    sums = tile_sums(op, val, wgt, step, block, live, segments)
    sums = exchange(sums)
    return recurrence(sums, transition, predicted_precision, starting_mean)


def solution(mesh):
    both = ("tm", "sensor")
    in_specs = (P(both, None, None), P(both, None), P(both, None), P(both), P(both), P(both), P(), P(), P())
    out_specs = (P("tm", None), P("tm", None))
    return jax.shard_map(shards, mesh=mesh, in_specs=in_specs, out_specs=out_specs, check_vma=False)
```

time: 741 us -> 79.3 us (0.11)
  matrix products: 313 us -> 0 us
  waiting for transfers between devices: 279 us -> 0 us
  Pallas kernels: 0 us -> 70.8 us
  blocking collectives: 66.3 us -> 0 us
  local copies, waits for them, and re-layouts: 48.4 us -> 7.51 us
  between operations: 14.7 us -> 0.71 us
  other arithmetic: 11 us -> 0 us
    dot_general x125 -> x0, matrix products: 313 us -> none  [the longest x64 141 us: compose_maps(): jnp.dot(later[0], earlier[1], precision=top_precision) + later[1]]
    all_gather x2 -> x0, waiting for transfers between devices: 174 us -> none  [prefix(): everything = jax.tree.map(lambda part: lax.all_gather(part, axis), shard)]
    unnamed x4 -> x0, waiting for transfers between devices: 105 us -> none
    pallas_call x0 -> x3, Pallas kernels: none -> 70.8 us  [the longest x1 38.6 us: recurrence(): pl.pallas_call(recurrence_kernel, out_shape=(shape, shape), in_specs=[vme...]
    all_gather x2 -> x0, blocking collectives: 53 us -> none  [prefix(): everything = jax.tree.map(lambda part: lax.all_gather(part, axis), shard)]
    while x40 -> x0, local copies, waits for them, and re-layouts: 39.9 us -> none
    psum x1 -> x0, blocking collectives: 13.3 us -> none  [shards(): gathered = lax.psum(gathered, 'sensor')]
    reduce_sum x1 -> x0, other arithmetic: 8.28 us -> none  [shards(): tile_curv = jnp.sum(squared * live_weight[:, :, None], axis=1)]
  transfers between devices with their start and end apart: 3 -> 0, of which waited for: 3 -> 0; matrix products, arithmetic and copies ran while one was open for 0% -> 0% of each run, Pallas kernels for 0% -> 0%
where the time goes in v1:
time: 79.3 us; the launch traced here: 79 us
  Pallas kernels  70.8 us (89%)
  local copies, waits for them, and re-layouts  7.51 us (9%)
    pallas_call x1, Pallas kernels, recurrence(): pl.pallas_call(recurrence_kernel, out_shape=(shape, shape), in_specs=[vme...  38.6 us
    pallas_call x1, Pallas kernels, exchange(): pl.pallas_call(exchange_kernel, out_shape=jax.ShapeDtypeStruct(sums.shape...  28.5 us
    unnamed x19, local copies, waits for them, and re-layouts  7.51 us
    pallas_call x1, Pallas kernels, tile_sums(): pl.pallas_call(functools.partial(tile_kernel, steps), grid=(steps,), out_...  3.74 us

profile of v1, /device:TPU:1, one launch (start us, length us, event | category | flops | bytes accessed | tf_op | source)
XLA Modules:
  0.0 79.0 jit_solution(1546039158981548320)
XLA Ops:
  0.6 0.0 copy-start.5
  0.6 0.0 copy-start.4
  0.7 0.0 copy-start
  0.7 3.4 %copy-done = bf16[256,128,128]{2,1,0:T(8,128)(2,1)S(1)} copy-done((bf16[256,128,128]{2,1,0:T(8,128)(2,1)S(1)}, bf16[256,128,128]{2,1,0:T(8,128)(2,1)}, u32[]{:S(2)}) %copy-start) | copy-done | bytes 8388632
  4.0 0.0 copy-start.2
  4.0 0.9 %copy-done.2 = f32[256,128]{1,0:T(8,128)S(1)} copy-done((f32[256,128]{1,0:T(8,128)S(1)}, f32[256,128]{1,0:T(8,128)}, u32[]{:S(2)}) %copy-start.2) | copy-done | bytes 131096
  5.0 0.0 copy-start.3
  5.0 0.8 %copy-done.3 = bf16[256,128]{1,0:T(8,128)(2,1)S(1)} copy-done((bf16[256,128]{1,0:T(8,128)(2,1)S(1)}, bf16[256,128]{1,0:T(8,128)(2,1)}, u32[]{:S(2)}) %copy-start.3) | copy-done | bytes 65560
  5.8 0.0 copy-start.6
  5.8 0.7 copy-done.6
  6.5 0.0 copy-start.7
  6.5 0.7 copy-done.7
  7.2 0.0 copy-start.8
  7.2 0.7 copy-done.8
  7.8 0.0 copy-start.1
  7.8 3.7 %shard_map.104.in_ref = f32[1024,128]{1,0:T(8,128)S(1)} custom-call(bf16[256,128,128]{2,1,0:T(8,128)(2,1)S(1)} %copy-done, bf16[256,128]{1,0:T(8,128)(2,1)S(1)} %copy-done.3, f32[256,128]{1,0:T(8,128)S(1)} %copy-done.2, s32[1,256]{1,0:T(1,128)S(1)} %bitcast.9, s32[1,256]{1,0:T(1,128)S(1)} %bitcast.10, s32[1,256]{1,0:T(1,128)S(1)} %bitcast.11), custom_call_target="tpu_custom_call" | custom-call | tf_op jit(solution)/shard_map/pallas_call | solution.py:78
  11.6 28.5 %shard_map.105.sums_ref = f32[1024,128]{1,0:T(8,128)S(1)} custom-call(f32[1024,128]{1,0:T(8,128)S(1)} %shard_map.104.in_ref), custom_call_target="tpu_custom_call" | custom-call | tf_op jit(solution)/shard_map/pallas_call | solution.py:207
  40.1 0.0 copy-done.1
  40.1 0.3 copy.11
  40.5 0.0 copy-done.5
  40.5 0.0 copy-done.4
  40.5 38.6 %shard_map.106 = (f32[4,512]{1,0:T(4,128)}, f32[4,512]{1,0:T(4,128)}) custom-call(f32[1024,128]{1,0:T(8,128)S(1)} %shard_map.105.sums_ref, f32[512,512]{1,0:T(8,128)S(1)} %copy-done.1, f32[512,512]{1,0:T(8,128)S(1)} %bitcast.6, f32[4,128]{1,0:T(4,128)S(1)} %bitcast.7, f32[4,128]{1,0:T(4,128)S(1)} %bitcast.8), custom_call_target="tpu_custom_call" | custom-call | tf_op jit(solution)/shard_map/pallas_call | solution.py:330
Async XLA Ops:
  0.6 39.8 %copy-start.5 = (f32[512]{0:T(512)S(1)}, f32[512]{0:T(512)}, u32[]{:S(2)}) copy-start(f32[512]{0:T(512)} %param.17) | copy-start | bytes 6148
  0.6 39.8 %copy-start.4 = (f32[512]{0:T(512)S(1)}, f32[512]{0:T(512)}, u32[]{:S(2)}) copy-start(f32[512]{0:T(512)} %param.16) | copy-start | bytes 6148
  0.7 3.4 %copy-start = (bf16[256,128,128]{2,1,0:T(8,128)(2,1)S(1)}, bf16[256,128,128]{2,1,0:T(8,128)(2,1)}, u32[]{:S(2)}) copy-start(bf16[256,128,128]{2,1,0:T(8,128)(2,1)} %op_ref.1) | copy-start | bytes 25165828
  4.0 0.9 %copy-start.2 = (f32[256,128]{1,0:T(8,128)S(1)}, f32[256,128]{1,0:T(8,128)}, u32[]{:S(2)}) copy-start(f32[256,128]{1,0:T(8,128)} %wgt_ref.1) | copy-start | bytes 393220
  5.0 0.8 %copy-start.3 = (bf16[256,128]{1,0:T(8,128)(2,1)S(1)}, bf16[256,128]{1,0:T(8,128)(2,1)}, u32[]{:S(2)}) copy-start(bf16[256,128]{1,0:T(8,128)(2,1)} %val_ref.1) | copy-start | bytes 196612
  5.8 0.7 copy-start.6
  6.5 0.7 copy-start.7
  7.2 0.7 copy-start.8
  7.8 32.3 %copy-start.1 = (f32[512,512]{1,0:T(8,128)S(1)}, f32[512,512]{1,0:T(8,128)}, u32[]{:S(2)}) copy-start(f32[512,512]{1,0:T(8,128)} %tran_ref.1) | copy-start | bytes 3145732

commit v2 on v1

v2 whole, which is shorter than its diff:
```python
import functools

import jax
import jax.numpy as jnp
from jax import lax
from jax.experimental import pallas as pl
from jax.experimental.pallas import tpu as pltpu
from jax.sharding import PartitionSpec as P

MESH = pl.DeviceIdType.MESH
TILE = 128
GROUPS = (("c",), ("x", "y", "z"))
SIZES = {"c": 2, "x": 4, "y": 4, "z": 4}
CHUNK = 128
VMEM = 60 << 20
F32, BF16 = jnp.float32, jnp.bfloat16


def parts(value):
    upper = value.astype(BF16)
    return upper, (value - upper.astype(F32)).astype(BF16)


def coordinates():
    tm = lax.axis_index("tm")
    return {
        "c": lax.rem(tm, 2),
        "x": lax.rem(lax.div(tm, 2), 4),
        "y": lax.div(tm, 8),
        "z": lax.axis_index("sensor"),
    }


def device_of(at):
    return (at["y"] * 8 + at["x"] * 2 + at["c"], at["z"])


def size_of(group):
    size = 1
    for axis in group:
        size *= SIZES[axis]
    return size


def member(mine, group, offset):
    at = dict(mine)
    for axis in group:
        at[axis] = lax.rem(mine[axis] + lax.rem(offset, SIZES[axis]), SIZES[axis])
        offset = lax.div(offset, SIZES[axis])
    return at


def index_in(group, at):
    index, scale = 0, 1
    for axis in group:
        index = index + at[axis] * scale
        scale *= SIZES[axis]
    return index


def greet_all(mine):
    barrier = pltpu.get_barrier_semaphore()
    for group in GROUPS:

        def greet(offset, carry, group=group):
            to = device_of(member(mine, group, offset))
            pl.semaphore_signal(barrier, inc=1, device_id=to, device_id_type=MESH)
            return carry

        lax.fori_loop(1, size_of(group), greet, 0)


def wait_all():
    pl.semaphore_wait(pltpu.get_barrier_semaphore(), sum(size_of(group) - 1 for group in GROUPS))


def exchange(mine, source, out_ref, works, boxes, send_in, recv_in, send_out, recv_out):
    count = len(GROUPS)
    start, starts = 0, []
    for stage, group in enumerate(GROUPS):
        size = size_of(group)
        rows = source.shape[0] // size
        box = boxes[stage]

        def give(offset, carry, source=source, group=group, rows=rows, box=box, stage=stage):
            to = member(mine, group, offset)
            pltpu.make_async_remote_copy(
                src_ref=source.at[pl.ds(pl.multiple_of(index_in(group, to) * rows, 8), rows)],
                dst_ref=box.at[pl.ds(pl.multiple_of((offset - 1) * rows, 8), rows)],
                send_sem=send_in.at[stage],
                recv_sem=recv_in.at[stage],
                device_id=device_of(to),
                device_id_type=MESH,
            ).start()
            return carry

        lax.fori_loop(1, size, give, 0)
        pltpu.make_async_copy(box, box, recv_in.at[stage]).wait()
        me = index_in(group, mine) * rows
        own = source[pl.ds(pl.multiple_of(me, 8), rows), :]
        works[stage][...] = own + jnp.sum(box[...].reshape(size - 1, rows, TILE), axis=0)
        start = start + me
        starts.append(start)
        source = works[stage]

    last = source.shape[0]
    out_ref[pl.ds(pl.multiple_of(start, 8), last), :] = source[...]
    for stage in reversed(range(count)):
        group = GROUPS[stage]
        rows = works[stage].shape[0]
        piece = out_ref.at[pl.ds(pl.multiple_of(starts[stage], 8), rows)]

        def spread(offset, carry, group=group, piece=piece, stage=stage):
            pltpu.make_async_remote_copy(
                src_ref=piece,
                dst_ref=piece,
                send_sem=send_out.at[stage],
                recv_sem=recv_out.at[stage],
                device_id=device_of(member(mine, group, offset)),
                device_id_type=MESH,
            ).start()
            return carry

        lax.fori_loop(1, size_of(group), spread, 0)
        pltpu.make_async_copy(boxes[stage], boxes[stage], recv_out.at[stage]).wait()
    for stage in range(count):
        pltpu.make_async_copy(boxes[stage], boxes[stage], send_in.at[stage]).wait()
        pltpu.make_async_copy(boxes[stage], boxes[stage], send_out.at[stage]).wait()


def tile_kernel(
    steps, op_ref, val_ref, wgt_ref, step_ref, block_ref, live_ref, out_ref, lhs, info, curv, local, all_sums, *scratch
):
    count = len(GROUPS)
    k = pl.program_id(0)
    tiles = wgt_ref.shape[0]
    mine = coordinates()

    @pl.when(k == 0)
    def _():
        greet_all(mine)
        for half in range(tiles // TILE):
            rows = pl.ds(half * TILE, TILE)
            live_count = live_ref[:, half * TILE : (half + 1) * TILE].astype(F32)
            live_count = jnp.transpose(jnp.broadcast_to(live_count, (TILE, TILE)))
            columns = lax.broadcasted_iota(jnp.int32, (TILE, TILE), 1).astype(F32)
            live = jnp.where(columns < live_count, wgt_ref[rows, :], 0.0)
            weighted = (live * val_ref[rows, :].astype(F32)).astype(BF16).astype(F32)
            upper = live.astype(BF16).astype(F32)
            lower = live - upper
            for kind, value in enumerate((weighted, upper, lower, jnp.zeros_like(live))):
                lhs[pl.ds(half * TILE // 8, TILE // 8), kind * 8 : (kind + 1) * 8, :] = value.reshape(
                    TILE // 8, 8, TILE
                )

    each = op_ref.shape[0]
    place = lax.broadcasted_iota(jnp.int32, (8, TILE), 0)
    for group in range(each // 8):
        left = lhs[k * (each // 8) + group].astype(BF16)
        info_sum = jnp.zeros((8, TILE), F32)
        curv_sum = jnp.zeros((8, TILE), F32)
        for j in range(8):
            op = op_ref[group * 8 + j]
            both = jnp.concatenate([op, op * op], axis=1)
            got = jnp.dot(left, both, preferred_element_type=F32)
            info_sum = jnp.where(place == j, got[0:8, :TILE], info_sum)
            curv_sum = jnp.where(place == j, got[8:16, TILE:] + got[16:24, TILE:], curv_sum)
        at = pl.ds(pl.multiple_of(k * each + group * 8, 8), 8)
        info[at, :] = info_sum
        curv[at, :] = curv_sum

    @pl.when(k == steps - 1)
    def _():
        segments = out_ref.shape[0] // 2
        ids = step_ref[...] * 4 + block_ref[...]
        targets = lax.broadcasted_iota(jnp.int32, (segments, tiles), 0)
        onehot = jnp.where(targets == ids, 1.0, 0.0).astype(BF16)
        stack = jnp.concatenate(parts(info[...]) + parts(curv[...]), axis=1)
        sums = jnp.dot(onehot, stack, preferred_element_type=F32)
        local[:segments, :] = sums[:, :TILE] + sums[:, TILE : 2 * TILE]
        local[segments:, :] = sums[:, 2 * TILE : 3 * TILE] + sums[:, 3 * TILE :]
        wait_all()
        exchange(mine, local, all_sums, scratch[:count], scratch[count : 2 * count], *scratch[2 * count :])
        out_ref[...] = all_sums[...]


def summed(op, val, wgt, step, block, live, segments):
    tiles = op.shape[0]
    steps = 8
    each = tiles // steps
    rows, works, boxes = 2 * segments, [], []
    for group in GROUPS:
        size = size_of(group)
        rows //= size
        works.append(pltpu.VMEM((rows, TILE), F32))
        boxes.append(pltpu.VMEM(((size - 1) * rows, TILE), F32))

    def whole(*shape):
        return pl.BlockSpec(shape, lambda k: (0,) * len(shape))

    return pl.pallas_call(
        functools.partial(tile_kernel, steps),
        grid=(steps,),
        out_shape=jax.ShapeDtypeStruct((2 * segments, TILE), F32),
        in_specs=[
            pl.BlockSpec((each, TILE, TILE), lambda k: (k, 0, 0)),
            whole(tiles, TILE),
            whole(tiles, TILE),
            whole(1, tiles),
            whole(1, tiles),
            whole(1, tiles),
        ],
        out_specs=whole(2 * segments, TILE),
        scratch_shapes=[
            pltpu.VMEM((tiles // 8, 32, TILE), F32),
            pltpu.VMEM((tiles, TILE), F32),
            pltpu.VMEM((tiles, TILE), F32),
            pltpu.VMEM((2 * segments, TILE), F32),
            pltpu.VMEM((2 * segments, TILE), F32),
            *works,
            *boxes,
        ]
        + [pltpu.SemaphoreType.DMA((len(GROUPS),))] * 4,
        compiler_params=pltpu.CompilerParams(
            collective_id=0, has_side_effects=True, vmem_limit_bytes=VMEM
        ),
    )(op, val, wgt, step.reshape(1, -1), block.reshape(1, -1), live.reshape(1, -1))


def recurrence_kernel(
    sums_ref, tran_ref, flip_ref, prec_ref, start_ref, filt_ref, smooth_ref,
    gain, drive, drive_on, drive_back, gain_col, diff_col, diff_row, filt_row, extra_row, filt_col, extra_col,
):
    segments = sums_ref.shape[0] // 2
    times = segments // 4
    half = times // 2
    width = tran_ref.shape[0]
    chunks = width // CHUNK
    first = lax.axis_index("tm") * 2

    pp = prec_ref[...]
    pp = jnp.concatenate([pp, pp], axis=0)[None]
    observed = sums_ref[segments:, :].reshape(segments // 8, 8, TILE)
    inform = sums_ref[:segments, :].reshape(segments // 8, 8, TILE)
    inverse = 1.0 / (pp + observed)
    gain[...] = (pp * inverse).reshape(segments, TILE)
    drive[...] = (inform * inverse).reshape(segments, TILE)
    for b in range(4):
        rows = slice(b * TILE, (b + 1) * TILE)
        g = jnp.transpose(gain[pl.ds(b, times, 4), :])
        for i in range(half):
            gain_col[i, rows, :] = jnp.broadcast_to(g[:, 2 * i : 2 * i + 1], (TILE, TILE))

    even_drive = jnp.concatenate([drive[pl.ds(b, half, 8), :] for b in range(4)], axis=1)
    upper, lower = parts(even_drive)
    both = jnp.concatenate([upper, lower], axis=0)
    for ref, moved in ((flip_ref, drive_on), (tran_ref, drive_back)):
        high, low = parts(ref[...])
        main = jnp.dot(both, high, preferred_element_type=F32)
        total = main[:half] + (main[half:] + jnp.dot(upper, low, preferred_element_type=F32))
        for b in range(4):
            moved[b] = total[:, b * TILE : (b + 1) * TILE]

    def part(ref, c, *lead):
        return ref[(*lead, slice(c * CHUNK, (c + 1) * CHUNK), slice(None))].reshape(CHUNK // 8, 8, TILE)

    def block(ref, c, b):
        return ref[c * CHUNK : (c + 1) * CHUNK, b * TILE : (b + 1) * TILE].reshape(CHUNK // 8, 8, TILE)

    def row_to_col(ref, wide, c):
        total = block(ref, c, 0) * wide[0]
        for b in range(1, 4):
            total += block(ref, c, b) * wide[b]
        return jnp.sum(total, axis=2, keepdims=True)

    def gather(ref, col, c, sums):
        for b in range(4):
            sums[b].append(jnp.sum(block(ref, c, b) * col, axis=0))

    def finish(pieces):
        while len(pieces) > 1:
            pieces = [sum(pieces[k : k + 2]) for k in range(0, len(pieces), 2)]
        return jnp.sum(pieces[0], axis=0, keepdims=True)

    def spread(row):
        return [jnp.broadcast_to(r, (8, TILE))[None] for r in row]

    def forward(keep, i, row):
        even, odd = 2 * i, 2 * i + 1
        wide = spread(row)
        sums = [[] for _ in range(4)]
        for c in range(chunks):
            rows = slice(c * CHUNK, (c + 1) * CHUNK)
            bare = row_to_col(tran_ref, wide, c)
            col = part(gain_col, c, i) * bare
            gather(flip_ref, col, c, sums)
            diff_col[i, rows, :] = (col - bare).reshape(CHUNK, TILE)
            if keep is not None:
                filt_col[keep, rows, :] = col.reshape(CHUNK, TILE)
        out = []
        for b in range(4):
            at = pl.ds(4 * odd + b, 1)
            moved = finish(sums[b]) + drive_on[b, pl.ds(i, 1), :]
            value = gain[at, :] * moved + drive[at, :]
            diff_row[at, :] = value - moved
            filt_row[at, :] = value
            out.append(value)
        return tuple(out)

    row = tuple(start_ref[b : b + 1, :] for b in range(4))
    plain = functools.partial(forward, None)
    row = lax.fori_loop(0, first, plain, row)
    row = forward(0, first, row)
    row = forward(1, first + 1, row)
    row = lax.fori_loop(first + 2, half, plain, row)

    def step_back(odd, sums, moved):
        back = []
        for b in range(4):
            at = pl.ds(4 * odd + b, 1)
            value = gain[at, :] * (finish(sums[b]) + moved[b])
            extra_row[at, :] = value
            back.append(value + diff_row[at, :])
        return tuple(back)

    wide = spread(row)
    sums = [[] for _ in range(4)]
    for c in range(chunks):
        gather(tran_ref, -row_to_col(tran_ref, wide, c), c, sums)
    gain[4 * (times - 1) :, :] = jnp.zeros((4, TILE), F32)
    row = step_back(times - 1, sums, [0.0] * 4)

    def backward(keep, i, row):
        wide = spread(row)
        sums = [[] for _ in range(4)]
        for c in range(chunks):
            col = part(gain_col, c, i) * row_to_col(flip_ref, wide, c)
            if keep is not None:
                extra_col[keep, c * CHUNK : (c + 1) * CHUNK, :] = col.reshape(CHUNK, TILE)
            if keep != 0:
                gather(tran_ref, col + part(diff_col, c, i), c, sums)
        if keep == 0:
            return row
        moved = [drive_back[b, pl.ds(i, 1), :] for b in range(4)]
        return step_back(2 * i - 1, sums, moved)

    row = lax.fori_loop(0, half - 2 - first, lambda n, r: backward(None, half - 1 - n, r), row)
    row = backward(1, first + 1, row)
    backward(0, first, row)

    eye = lax.broadcasted_iota(jnp.int32, (TILE, TILE), 0) == lax.broadcasted_iota(jnp.int32, (TILE, TILE), 1)
    for keep in range(2):
        for b in range(4):
            lane = slice(b * TILE, (b + 1) * TILE)
            f = jnp.sum(jnp.where(eye, filt_col[keep, lane, :], 0.0), axis=0, keepdims=True)
            f = f + drive[pl.ds(8 * (first + keep) + b, 1), :]
            e = jnp.sum(jnp.where(eye, extra_col[keep, lane, :], 0.0), axis=0, keepdims=True)
            filt_ref[2 * keep : 2 * keep + 1, lane] = f
            smooth_ref[2 * keep : 2 * keep + 1, lane] = f + e
            at = pl.ds(4 * (2 * (first + keep) + 1) + b, 1)
            f = filt_row[at, :]
            filt_ref[2 * keep + 1 : 2 * keep + 2, lane] = f
            smooth_ref[2 * keep + 1 : 2 * keep + 2, lane] = f + extra_row[at, :]


def recurrence(sums, transition, predicted_precision, starting_mean):
    segments = sums.shape[0] // 2
    width = transition.shape[0]
    times = segments // 4
    vmem = pl.BlockSpec(memory_space=pltpu.VMEM)
    shape = jax.ShapeDtypeStruct((4, width), F32)
    return pl.pallas_call(
        recurrence_kernel,
        out_shape=(shape, shape),
        in_specs=[vmem] * 5,
        out_specs=(vmem, vmem),
        scratch_shapes=[
            pltpu.VMEM((segments, TILE), F32),
            pltpu.VMEM((segments, TILE), F32),
            pltpu.VMEM((4, times // 2, TILE), F32),
            pltpu.VMEM((4, times // 2, TILE), F32),
            pltpu.VMEM((times // 2, width, TILE), F32),
            pltpu.VMEM((times // 2, width, TILE), F32),
            pltpu.VMEM((segments, TILE), F32),
            pltpu.VMEM((segments, TILE), F32),
            pltpu.VMEM((segments, TILE), F32),
            pltpu.VMEM((2, width, TILE), F32),
            pltpu.VMEM((2, width, TILE), F32),
        ],
        compiler_params=pltpu.CompilerParams(vmem_limit_bytes=48 << 20),
    )(
        sums,
        transition,
        transition.T,
        predicted_precision.reshape(4, TILE),
        starting_mean.reshape(4, TILE),
    )


def shards(op, val, wgt, step, block, live, transition, predicted_precision, starting_mean):
    segments = 4 * 4 * lax.axis_size("tm")
    sums = summed(op, val, wgt, step, block, live, segments)
    return recurrence(sums, transition, predicted_precision, starting_mean)


def solution(mesh):
    both = ("tm", "sensor")
    in_specs = (P(both, None, None), P(both, None), P(both, None), P(both), P(both), P(both), P(), P(), P())
    out_specs = (P("tm", None), P("tm", None))
    return jax.shard_map(shards, mesh=mesh, in_specs=in_specs, out_specs=out_specs, check_vma=False)
```

time: 79.3 us -> 64.3 us (0.81)
  Pallas kernels: 70.8 us -> 61.9 us
  local copies, waits for them, and re-layouts: 7.51 us -> 1.38 us
    pallas_call x1, Pallas kernels: 38.6 us -> 28.5 us  [recurrence(): pl.pallas_call(recurrence_kernel, out_shape=(shape, shape), in_specs=[vme...]
    unnamed x19 -> x9, local copies, waits for them, and re-layouts: 7.51 us -> 1.38 us
    pallas_call x2 -> x1, Pallas kernels: 32.3 us -> 33.4 us  [summed(): pl.pallas_call(functools.partial(tile_kernel, steps), grid=(steps,), out_...]
where the time goes in v2:
time: 64.3 us; the launch traced here: 64 us
  Pallas kernels  61.9 us (96%)
  local copies, waits for them, and re-layouts  1.38 us (2%)
  between operations  0.7 us (1%)
    pallas_call x1, Pallas kernels, summed(): pl.pallas_call(functools.partial(tile_kernel, steps), grid=(steps,), out_...  33.4 us
    pallas_call x1, Pallas kernels, recurrence(): pl.pallas_call(recurrence_kernel, out_shape=(shape, shape), in_specs=[vme...  28.5 us
    unnamed x9, local copies, waits for them, and re-layouts  1.38 us

profile of v2, /device:TPU:1, one launch (start us, length us, event | category | flops | bytes accessed | tf_op | source)
XLA Modules:
  0.0 64.0 jit_solution(3265094405241791206)
XLA Ops:
  0.6 0.0 copy-start
  0.6 0.0 copy-start.3
  0.7 0.0 copy-start.2
  0.7 33.4 %shard_map.104.sums_ref = f32[1024,128]{1,0:T(8,128)} custom-call(bf16[256,128,128]{2,1,0:T(8,128)(2,1)} %op_ref.1, bf16[256,128]{1,0:T(8,128)(2,1)} %val_ref.1, f32[256,128]{1,0:T(8,128)} %wgt_ref.1, s32[1,256]{1,0:T(1,128)} %bitcast.9, s32[1,256]{1,0:T(1,128)} %bitcast.10, s32[1,256]{1,0:T(1,128)} %bitcast.11), custom_call_target="tpu_custom_call" | custom-call | tf_op jit(solution)/shard_map/pallas_call | solution.py:201
  34.1 0.0 copy-done
  34.1 0.3 copy.11
  34.4 0.0 copy-done.3
  34.4 0.0 copy-done.2
  34.4 0.0 copy-start.1
  34.5 1.0 %copy-done.1 = f32[1024,128]{1,0:T(8,128)S(1)} copy-done((f32[1024,128]{1,0:T(8,128)S(1)}, f32[1024,128]{1,0:T(8,128)}, u32[]{:S(2)}) %copy-start.1) | copy-done | bytes 524312
  35.5 28.5 %shard_map.105 = (f32[4,512]{1,0:T(4,128)}, f32[4,512]{1,0:T(4,128)}) custom-call(f32[1024,128]{1,0:T(8,128)S(1)} %copy-done.1, f32[512,512]{1,0:T(8,128)S(1)} %copy-done, f32[512,512]{1,0:T(8,128)S(1)} %bitcast.6, f32[4,128]{1,0:T(4,128)S(1)} %bitcast.7, f32[4,128]{1,0:T(4,128)S(1)} %bitcast.8), custom_call_target="tpu_custom_call" | custom-call | tf_op jit(solution)/shard_map/pallas_call | solution.py:372
Async XLA Ops:
  0.6 33.4 %copy-start = (f32[512,512]{1,0:T(8,128)S(1)}, f32[512,512]{1,0:T(8,128)}, u32[]{:S(2)}) copy-start(f32[512,512]{1,0:T(8,128)} %tran_ref.1) | copy-start | bytes 3145732
  0.6 33.8 %copy-start.3 = (f32[512]{0:T(512)S(1)}, f32[512]{0:T(512)}, u32[]{:S(2)}) copy-start(f32[512]{0:T(512)} %param.17) | copy-start | bytes 6148
  0.7 33.8 %copy-start.2 = (f32[512]{0:T(512)S(1)}, f32[512]{0:T(512)}, u32[]{:S(2)}) copy-start(f32[512]{0:T(512)} %param.16) | copy-start | bytes 6148
  34.4 1.0 %copy-start.1 = (f32[1024,128]{1,0:T(8,128)S(1)}, f32[1024,128]{1,0:T(8,128)}, u32[]{:S(2)}) copy-start(f32[1024,128]{1,0:T(8,128)} %shard_map.104.sums_ref) | copy-start | bytes 1572868

commit v3 on v2

v3 whole, which is shorter than its diff:
```python
import functools
import itertools

import jax
import jax.numpy as jnp
from jax import lax
from jax.experimental import pallas as pl
from jax.experimental.pallas import tpu as pltpu
from jax.sharding import PartitionSpec as P

MESH = pl.DeviceIdType.MESH
TILE = 128
GROUPS = (("c",), ("y", "x", "z"))
SIZES = {"c": 2, "x": 4, "y": 4, "z": 4}
CHUNK = 128
PARTS = 8
F32, BF16 = jnp.float32, jnp.bfloat16


def parts(value):
    upper = value.astype(BF16)
    return upper, (value - upper.astype(F32)).astype(BF16)


def coordinates():
    tm = lax.axis_index("tm")
    mine = {
        "c": lax.rem(tm, 2),
        "x": lax.rem(lax.div(tm, 2), 4),
        "y": lax.div(tm, 8),
        "z": lax.axis_index("sensor"),
    }
    return {
        axis: [mine[axis]] + [lax.rem(mine[axis] + k, size) for k in range(1, size)]
        for axis, size in SIZES.items()
    }


def hops(offsets):
    return sum(min(offset, 4 - offset) for offset in offsets)


def team(group):
    every = list(itertools.product(*[range(SIZES[axis]) for axis in group]))[1:]
    return sorted(every, key=hops, reverse=True)


def size_of(group):
    return len(team(group)) + 1


def member(near, group, offsets):
    at = {axis: near[axis][0] for axis in SIZES}
    for axis, offset in zip(group, offsets):
        at[axis] = near[axis][offset]
    return at


def device_of(at):
    return (at["y"] * 8 + at["x"] * 2 + at["c"], at["z"])


def index_in(group, at):
    index = 0
    for axis in group:
        index = index * SIZES[axis] + at[axis]
    return index


def greet_all(near):
    barrier = pltpu.get_barrier_semaphore()
    for group in GROUPS:
        for offsets in team(group):
            to = device_of(member(near, group, offsets))
            pl.semaphore_signal(barrier, inc=1, device_id=to, device_id_type=MESH)


def wait_all():
    pl.semaphore_wait(pltpu.get_barrier_semaphore(), sum(size_of(group) - 1 for group in GROUPS))


def scatter(near, source, stage, rows, box, send, recv):
    group = GROUPS[stage]
    for k, offsets in enumerate(team(group)):
        to = member(near, group, offsets)
        pltpu.make_async_remote_copy(
            src_ref=source.at[pl.ds(pl.multiple_of(index_in(group, to) * rows, 8), rows)],
            dst_ref=box.at[pl.ds(k * rows, rows)],
            send_sem=send.at[stage],
            recv_sem=recv.at[stage],
            device_id=device_of(to),
            device_id_type=MESH,
        ).start()


def spread(near, out_ref, start, stage, rows, send, recv):
    group = GROUPS[stage]
    piece = out_ref.at[pl.ds(pl.multiple_of(start, 8), rows)]
    for offsets in team(group):
        pltpu.make_async_remote_copy(
            src_ref=piece,
            dst_ref=piece,
            send_sem=send.at[stage],
            recv_sem=recv.at[stage],
            device_id=device_of(member(near, group, offsets)),
            device_id_type=MESH,
        ).start()


def wait_bytes(box, sem):
    pltpu.make_async_copy(box, box, sem).wait()


def exchange(near, source, out_ref, works, boxes, send_in, recv_in, send_out, recv_out, meanwhile):
    count = len(GROUPS)
    start, starts = 0, []
    for stage, group in enumerate(GROUPS):
        size = size_of(group)
        rows = source.shape[0] // size
        box = boxes[stage]
        scatter(near, source, stage, rows, box, send_in, recv_in)
        me = pl.multiple_of(index_in(group, {axis: near[axis][0] for axis in SIZES}) * rows, 8)
        if stage == count - 1:
            meanwhile()
        wait_bytes(box, recv_in.at[stage])
        own = source[pl.ds(me, rows), :]
        works[stage][...] = own + jnp.sum(box[...].reshape(size - 1, rows, TILE), axis=0)
        start = start + me
        starts.append(start)
        source = works[stage]

    out_ref[pl.ds(pl.multiple_of(start, 8), source.shape[0]), :] = source[...]
    for stage in reversed(range(count)):
        spread(near, out_ref, starts[stage], stage, works[stage].shape[0], send_out, recv_out)
        wait_bytes(boxes[stage], recv_out.at[stage])
    for stage in range(count):
        wait_bytes(boxes[stage], send_in.at[stage])
        wait_bytes(boxes[stage], send_out.at[stage])


def tile_kernel(
    op_ref, val_hbm, wgt_hbm, step_hbm, block_hbm, live_hbm, tran_hbm, prec_hbm, start_hbm,
    filt_ref, smooth_ref,
    out_ref, tran_ref, flip_ref, prec_ref, start_ref, tiles_ref, val_ref, wgt_ref, step_ref, block_ref, live_ref, lhs, info, curv, local, small_sem, tile_sem,
    *scratch,
):
    count = len(GROUPS)
    scratch, own = scratch[: 2 * count + 4], scratch[2 * count + 4 :]
    tiles = op_ref.shape[0]
    each = tiles // PARTS
    small = ((live_hbm, live_ref), (wgt_hbm, wgt_ref), (val_hbm, val_ref), (step_hbm, step_ref), (block_hbm, block_ref),
             (tran_hbm, tran_ref), (prec_hbm, prec_ref), (start_hbm, start_ref))
    small = [pltpu.make_async_copy(a, b, small_sem.at[k]) for k, (a, b) in enumerate(small)]
    for copy in small[:3]:
        copy.start()

    def load(k):
        at = pl.ds(pl.multiple_of(k * each, each), each)
        return pltpu.make_async_copy(op_ref.at[at], tiles_ref.at[at], tile_sem.at[k])

    for k in range(PARTS):
        load(k).start()
    for copy in small[3:]:
        copy.start()
    near = coordinates()
    greet_all(near)

    for copy in small[:3]:
        copy.wait()
    for half in range(tiles // TILE):
        rows = pl.ds(half * TILE, TILE)
        live_count = live_ref[:, half * TILE : (half + 1) * TILE].astype(F32)
        live_count = jnp.transpose(jnp.broadcast_to(live_count, (TILE, TILE)))
        columns = lax.broadcasted_iota(jnp.int32, (TILE, TILE), 1).astype(F32)
        live = jnp.where(columns < live_count, wgt_ref[rows, :], 0.0)
        weighted = (live * val_ref[rows, :].astype(F32)).astype(BF16).astype(F32)
        upper = live.astype(BF16).astype(F32)
        lower = live - upper
        for kind, value in enumerate((weighted, upper, lower, jnp.zeros_like(live))):
            lhs[pl.ds(half * TILE // 8, TILE // 8), kind * 8 : (kind + 1) * 8, :] = value.reshape(TILE // 8, 8, TILE)

    place = lax.broadcasted_iota(jnp.int32, (8, TILE), 0)

    def part_sums(k, carry):
        load(k).wait()
        for group in range(each // 8):
            left = lhs[k * (each // 8) + group].astype(BF16)
            info_sum = jnp.zeros((8, TILE), F32)
            curv_sum = jnp.zeros((8, TILE), F32)
            for j in range(8):
                op = tiles_ref[k * each + group * 8 + j]
                both = jnp.concatenate([op, op * op], axis=1)
                got = jnp.dot(left, both, preferred_element_type=F32)
                info_sum = jnp.where(place == j, got[0:8, :TILE], info_sum)
                curv_sum = jnp.where(place == j, got[8:16, TILE:] + got[16:24, TILE:], curv_sum)
            at = pl.ds(pl.multiple_of(k * each + group * 8, 8), 8)
            info[at, :] = info_sum
            curv[at, :] = curv_sum
        return carry

    lax.fori_loop(0, PARTS, part_sums, 0)

    for copy in small[3:5]:
        copy.wait()
    segments = out_ref.shape[0] // 2
    ids = step_ref[...] * 4 + block_ref[...]
    targets = lax.broadcasted_iota(jnp.int32, (segments, tiles), 0)
    onehot = jnp.where(targets == ids, 1.0, 0.0).astype(BF16)
    stack = jnp.concatenate(parts(info[...]) + parts(curv[...]), axis=1)
    sums = jnp.dot(onehot, stack, preferred_element_type=F32)
    inform = (sums[:, :TILE] + sums[:, TILE : 2 * TILE]).reshape(segments // 8, 1, 8, TILE)
    observed = (sums[:, 2 * TILE : 3 * TILE] + sums[:, 3 * TILE :]).reshape(segments // 8, 1, 8, TILE)
    local[...] = jnp.concatenate([inform, observed], axis=1).reshape(2 * segments, TILE)
    wait_all()

    def meanwhile():
        for copy in small[5:]:
            copy.wait()
        for i in range(tran_ref.shape[0] // TILE):
            for j in range(tran_ref.shape[0] // TILE):
                a, b = slice(i * TILE, (i + 1) * TILE), slice(j * TILE, (j + 1) * TILE)
                flip_ref[b, a] = jnp.transpose(tran_ref[a, b])

    exchange(near, local, out_ref, scratch[:count], scratch[count : 2 * count], *scratch[2 * count :], meanwhile)
    recurrence(out_ref, tran_ref, flip_ref, prec_ref, start_ref, filt_ref, smooth_ref, *own)


def recurrence(
    sums_ref, tran_ref, flip_ref, prec_ref, start_ref, filt_ref, smooth_ref,
    gain, drive, drive_on, drive_back, gain_col, diff_col, diff_row, filt_row, extra_row, filt_col, extra_col,
):
    segments = sums_ref.shape[0] // 2
    times = segments // 4
    half = times // 2
    width = tran_ref.shape[0]
    chunks = width // CHUNK
    first = lax.axis_index("tm") * 2

    pp = prec_ref[...]
    pp = jnp.concatenate([pp, pp], axis=0)[None]
    both = sums_ref[...].reshape(segments // 8, 2, 8, TILE)
    inform, observed = both[:, 0], both[:, 1]
    inverse = 1.0 / (pp + observed)
    gain[...] = (pp * inverse).reshape(segments, TILE)
    drive[...] = (inform * inverse).reshape(segments, TILE)
    for b in range(4):
        rows = slice(b * TILE, (b + 1) * TILE)
        g = jnp.transpose(gain[pl.ds(b, times, 4), :])
        for i in range(half):
            gain_col[i, rows, :] = jnp.broadcast_to(g[:, 2 * i : 2 * i + 1], (TILE, TILE))

    even_drive = jnp.concatenate([drive[pl.ds(b, half, 8), :] for b in range(4)], axis=1)
    upper, lower = parts(even_drive)
    both = jnp.concatenate([upper, lower], axis=0)
    for ref, moved in ((flip_ref, drive_on), (tran_ref, drive_back)):
        high, low = parts(ref[...])
        main = jnp.dot(both, high, preferred_element_type=F32)
        total = main[:half] + (main[half:] + jnp.dot(upper, low, preferred_element_type=F32))
        for b in range(4):
            moved[b] = total[:, b * TILE : (b + 1) * TILE]

    def part(ref, c, *lead):
        return ref[(*lead, slice(c * CHUNK, (c + 1) * CHUNK), slice(None))].reshape(CHUNK // 8, 8, TILE)

    def block(ref, c, b):
        return ref[c * CHUNK : (c + 1) * CHUNK, b * TILE : (b + 1) * TILE].reshape(CHUNK // 8, 8, TILE)

    def row_to_col(ref, wide, c):
        total = block(ref, c, 0) * wide[0]
        for b in range(1, 4):
            total += block(ref, c, b) * wide[b]
        return jnp.sum(total, axis=2, keepdims=True)

    def gather(ref, col, c, sums):
        for b in range(4):
            sums[b].append(jnp.sum(block(ref, c, b) * col, axis=0))

    def finish(pieces):
        while len(pieces) > 1:
            pieces = [sum(pieces[k : k + 2]) for k in range(0, len(pieces), 2)]
        return jnp.sum(pieces[0], axis=0, keepdims=True)

    def spread(row):
        return [jnp.broadcast_to(r, (8, TILE))[None] for r in row]

    def forward(keep, i, row):
        even, odd = 2 * i, 2 * i + 1
        wide = spread(row)
        sums = [[] for _ in range(4)]
        for c in range(chunks):
            rows = slice(c * CHUNK, (c + 1) * CHUNK)
            bare = row_to_col(tran_ref, wide, c)
            col = part(gain_col, c, i) * bare
            gather(flip_ref, col, c, sums)
            diff_col[i, rows, :] = (col - bare).reshape(CHUNK, TILE)
            if keep is not None:
                filt_col[keep, rows, :] = col.reshape(CHUNK, TILE)
        out = []
        for b in range(4):
            at = pl.ds(4 * odd + b, 1)
            moved = finish(sums[b]) + drive_on[b, pl.ds(i, 1), :]
            value = gain[at, :] * moved + drive[at, :]
            diff_row[at, :] = value - moved
            filt_row[at, :] = value
            out.append(value)
        return tuple(out)

    row = tuple(start_ref[b : b + 1, :] for b in range(4))
    plain = functools.partial(forward, None)
    row = lax.fori_loop(0, first, plain, row)
    row = forward(0, first, row)
    row = forward(1, first + 1, row)
    row = lax.fori_loop(first + 2, half, plain, row)

    def step_back(odd, sums, moved):
        back = []
        for b in range(4):
            at = pl.ds(4 * odd + b, 1)
            value = gain[at, :] * (finish(sums[b]) + moved[b])
            extra_row[at, :] = value
            back.append(value + diff_row[at, :])
        return tuple(back)

    wide = spread(row)
    sums = [[] for _ in range(4)]
    for c in range(chunks):
        gather(tran_ref, -row_to_col(tran_ref, wide, c), c, sums)
    gain[4 * (times - 1) :, :] = jnp.zeros((4, TILE), F32)
    row = step_back(times - 1, sums, [0.0] * 4)

    def backward(keep, i, row):
        wide = spread(row)
        sums = [[] for _ in range(4)]
        for c in range(chunks):
            col = part(gain_col, c, i) * row_to_col(flip_ref, wide, c)
            if keep is not None:
                extra_col[keep, c * CHUNK : (c + 1) * CHUNK, :] = col.reshape(CHUNK, TILE)
            if keep != 0:
                gather(tran_ref, col + part(diff_col, c, i), c, sums)
        if keep == 0:
            return row
        moved = [drive_back[b, pl.ds(i, 1), :] for b in range(4)]
        return step_back(2 * i - 1, sums, moved)

    row = lax.fori_loop(0, half - 2 - first, lambda n, r: backward(None, half - 1 - n, r), row)
    row = backward(1, first + 1, row)
    backward(0, first, row)

    eye = lax.broadcasted_iota(jnp.int32, (TILE, TILE), 0) == lax.broadcasted_iota(jnp.int32, (TILE, TILE), 1)
    for keep in range(2):
        for b in range(4):
            lane = slice(b * TILE, (b + 1) * TILE)
            f = jnp.sum(jnp.where(eye, filt_col[keep, lane, :], 0.0), axis=0, keepdims=True)
            f = f + drive[pl.ds(8 * (first + keep) + b, 1), :]
            e = jnp.sum(jnp.where(eye, extra_col[keep, lane, :], 0.0), axis=0, keepdims=True)
            filt_ref[2 * keep : 2 * keep + 1, lane] = f
            smooth_ref[2 * keep : 2 * keep + 1, lane] = f + e
            at = pl.ds(4 * (2 * (first + keep) + 1) + b, 1)
            f = filt_row[at, :]
            filt_ref[2 * keep + 1 : 2 * keep + 2, lane] = f
            smooth_ref[2 * keep + 1 : 2 * keep + 2, lane] = f + extra_row[at, :]


def smoother(op, val, wgt, step, block, live, transition, predicted_precision, starting_mean, segments):
    tiles = op.shape[0]
    width = transition.shape[0]
    times = segments // 4
    rows, works, boxes = 2 * segments, [], []
    for group in GROUPS:
        size = size_of(group)
        rows //= size
        works.append(pltpu.VMEM((rows, TILE), F32))
        boxes.append(pltpu.VMEM(((size - 1) * rows, TILE), F32))
    hbm, vmem = pl.BlockSpec(memory_space=pltpu.HBM), pl.BlockSpec(memory_space=pltpu.VMEM)
    shape = jax.ShapeDtypeStruct((4, width), F32)
    return pl.pallas_call(
        tile_kernel,
        out_shape=(shape, shape),
        in_specs=[hbm] * 9,
        out_specs=(vmem, vmem),
        scratch_shapes=[
            pltpu.VMEM((2 * segments, TILE), F32),
            pltpu.VMEM((width, width), F32),
            pltpu.VMEM((width, width), F32),
            pltpu.VMEM((4, TILE), F32),
            pltpu.VMEM((4, TILE), F32),
            pltpu.VMEM((tiles, TILE, TILE), BF16),
            pltpu.VMEM((tiles, TILE), BF16),
            pltpu.VMEM((tiles, TILE), F32),
            pltpu.VMEM((1, tiles), jnp.int32),
            pltpu.VMEM((1, tiles), jnp.int32),
            pltpu.VMEM((1, tiles), jnp.int32),
            pltpu.VMEM((tiles // 8, 32, TILE), F32),
            pltpu.VMEM((tiles, TILE), F32),
            pltpu.VMEM((tiles, TILE), F32),
            pltpu.VMEM((2 * segments, TILE), F32),
            pltpu.SemaphoreType.DMA((8,)),
            pltpu.SemaphoreType.DMA((PARTS,)),
            *works,
            *boxes,
            *[pltpu.SemaphoreType.DMA((len(GROUPS),))] * 4,
            pltpu.VMEM((segments, TILE), F32),
            pltpu.VMEM((segments, TILE), F32),
            pltpu.VMEM((4, times // 2, TILE), F32),
            pltpu.VMEM((4, times // 2, TILE), F32),
            pltpu.VMEM((times // 2, width, TILE), F32),
            pltpu.VMEM((times // 2, width, TILE), F32),
            pltpu.VMEM((segments, TILE), F32),
            pltpu.VMEM((segments, TILE), F32),
            pltpu.VMEM((segments, TILE), F32),
            pltpu.VMEM((2, width, TILE), F32),
            pltpu.VMEM((2, width, TILE), F32),
        ],
        compiler_params=pltpu.CompilerParams(
            collective_id=0, has_side_effects=True, vmem_limit_bytes=62 << 20
        ),
    )(
        op,
        val,
        wgt,
        step.reshape(1, -1),
        block.reshape(1, -1),
        live.reshape(1, -1),
        transition,
        predicted_precision.reshape(4, TILE),
        starting_mean.reshape(4, TILE),
    )


def shards(op, val, wgt, step, block, live, transition, predicted_precision, starting_mean):
    segments = 4 * 4 * lax.axis_size("tm")
    return smoother(
        op, val, wgt, step, block, live, transition, predicted_precision, starting_mean, segments
    )


def solution(mesh):
    both = ("tm", "sensor")
    in_specs = (P(both, None, None), P(both, None), P(both, None), P(both), P(both), P(both), P(), P(), P())
    out_specs = (P("tm", None), P("tm", None))
    return jax.shard_map(shards, mesh=mesh, in_specs=in_specs, out_specs=out_specs, check_vma=False)
```

time: 64.3 us -> 60.4 us (0.939)
  Pallas kernels: 61.9 us -> 56.9 us
  local copies, waits for them, and re-layouts: 1.38 us -> 2.59 us
    pallas_call x2 -> x1, Pallas kernels: 61.9 us -> 56.9 us  [smoother(): pl.pallas_call(tile_kernel, out_shape=(shape, shape), in_specs=[hbm] * 9,...]
    unnamed x9 -> x2, local copies, waits for them, and re-layouts: 1.38 us -> 2.59 us
where the time goes in v3:
time: 60.4 us; the launch traced here: 60.2 us
  Pallas kernels  56.9 us (94%)
  local copies, waits for them, and re-layouts  2.59 us (4%)
  between operations  0.64 us (1%)
    pallas_call x1, Pallas kernels, smoother(): pl.pallas_call(tile_kernel, out_shape=(shape, shape), in_specs=[hbm] * 9,...  56.9 us
    unnamed x2, local copies, waits for them, and re-layouts  2.59 us

profile of v3, /device:TPU:1, one launch (start us, length us, event | category | flops | bytes accessed | tf_op | source)
XLA Modules:
  0.0 60.2 jit_solution(18101406781522095439)
XLA Ops:
  0.6 56.9 %shard_map.104 = (f32[4,512]{1,0:T(4,128)}, f32[4,512]{1,0:T(4,128)}) custom-call(bf16[256,128,128]{2,1,0:T(8,128)(2,1)} %op_ref.1, bf16[256,128]{1,0:T(8,128)(2,1)} %val_hbm.1, f32[256,128]{1,0:T(8,128)} %wgt_hbm.1, s32[1,256]{1,0:T(1,128)} %bitcast.7, s32[1,256]{1,0:T(1,128)} %bitcast.8, s32[1,256]{1,0:T(1,128)} %bitcast.9, f32[512,512]{1,0:T(8,128)} %tran_hbm.1, ...), custom_call_target="tpu_custom_call" | custom-call | tf_op jit(solution)/shard_map/pallas_call | solution.py:376
  57.6 1.3 %copy.13 = f32[4,512]{1,0:T(4,128)} copy(f32[4,512]{1,0:T(4,128)} %get-tuple-element.4) | data formatting | bytes 16384
  58.9 1.3 %copy.14 = f32[4,512]{1,0:T(4,128)} copy(f32[4,512]{1,0:T(4,128)} %get-tuple-element.5) | data formatting | bytes 16384

commit v4 on v3

--- a/solution.py
+++ b/solution.py
@@ -10,7 +10,6 @@
 
 MESH = pl.DeviceIdType.MESH
 TILE = 128
-GROUPS = (("c",), ("y", "x", "z"))
 SIZES = {"c": 2, "x": 4, "y": 4, "z": 4}
 CHUNK = 128
 PARTS = 8
@@ -40,102 +39,146 @@
     return sum(min(offset, 4 - offset) for offset in offsets)
 
 
-def team(group):
-    every = list(itertools.product(*[range(SIZES[axis]) for axis in group]))[1:]
-    return sorted(every, key=hops, reverse=True)
-
-
-def size_of(group):
-    return len(team(group)) + 1
-
-
-def member(near, group, offsets):
-    at = {axis: near[axis][0] for axis in SIZES}
-    for axis, offset in zip(group, offsets):
-        at[axis] = near[axis][offset]
-    return at
-
-
-def device_of(at):
-    return (at["y"] * 8 + at["x"] * 2 + at["c"], at["z"])
-
-
-def index_in(group, at):
-    index = 0
-    for axis in group:
-        index = index * SIZES[axis] + at[axis]
-    return index
+PLANE = sorted(itertools.product(range(4), range(4)), key=hops, reverse=True)
+
+
+def device_of(y, x, z, core):
+    return (y * 8 + x * 2 + core, z)
+
+
+def chip_of(y, x, z):
+    return (y * 4 + x) * 4 + z
+
+
+def partners(near):
+    core, half = near["c"][0], lax.div(near["y"][0], 2)
+    for k, (dx, dz) in enumerate(PLANE):
+        for a in range(2):
+            yield 2 * core + a, near["x"][dx], near["z"][dz], half, k, (dx, dz) == (0, 0)
+
+
+def to_partners(near, act, at_home=None):
+    for y, x, z, core, k, close in partners(near):
+        if close:
+            pl.when(y != near["y"][0])(functools.partial(act, y, x, z, core, k))
+            if at_home is not None:
+                pl.when(y == near["y"][0])(functools.partial(at_home, y, x, z, core, k))
+        else:
+            act(y, x, z, core, k)
+
+
+def is_home(near):
+    return lax.div(near["y"][0], 2) == near["c"][0]
+
+
+def wait_bytes(ref, sem):
+    pltpu.make_async_copy(ref, ref, sem).wait()
+
+
+def wait_partners(near, box, sem):
+    rows = box.shape[0]
+    home = is_home(near)
+
+    @pl.when(home)
+    def _():
+        wait_bytes(box.at[pl.ds(0, rows - rows // 32)], sem)
+
+    @pl.when(jnp.logical_not(home))
+    def _():
+        wait_bytes(box, sem)
 
 
 def greet_all(near):
     barrier = pltpu.get_barrier_semaphore()
-    for group in GROUPS:
-        for offsets in team(group):
-            to = device_of(member(near, group, offsets))
-            pl.semaphore_signal(barrier, inc=1, device_id=to, device_id_type=MESH)
-
-
-def wait_all():
-    pl.semaphore_wait(pltpu.get_barrier_semaphore(), sum(size_of(group) - 1 for group in GROUPS))
-
-
-def scatter(near, source, stage, rows, box, send, recv):
-    group = GROUPS[stage]
-    for k, offsets in enumerate(team(group)):
-        to = member(near, group, offsets)
+    y, x, z = near["y"][0], near["x"][0], near["z"][0]
+    pl.semaphore_signal(barrier, inc=1, device_id=device_of(y, x, z, near["c"][1]), device_id_type=MESH)
+
+    def greet(y, x, z, core, k):
+        pl.semaphore_signal(barrier, inc=1, device_id=device_of(y, x, z, core), device_id_type=MESH)
+
+    to_partners(near, greet)
+
+
+def wait_all(near):
+    pl.semaphore_wait(pltpu.get_barrier_semaphore(), jnp.where(is_home(near), 32, 33))
+
+
+def exchange(near, source, out_ref, half_sum, pair_box, box, mine, twin, sems, meanwhile):
+    core, y, x, z = near["c"][0], near["y"][0], near["x"][0], near["z"][0]
+    sibling = device_of(y, x, z, near["c"][1])
+    half_rows = half_sum.shape[0]
+    rows = mine.shape[0]
+    here = chip_of(y, x, z)
+
+    def to_sibling(src, dst, k):
+        copy = pltpu.make_async_remote_copy(
+            src_ref=src,
+            dst_ref=dst,
+            send_sem=sems.at[2 * k],
+            recv_sem=sems.at[2 * k + 1],
+            device_id=sibling,
+            device_id_type=MESH,
+        )
+        copy.start()
+        return copy
+
+    kept = pl.multiple_of(core * half_rows, 8)
+    given = pl.multiple_of((1 - core) * half_rows, 8)
+    first = to_sibling(source.at[pl.ds(given, half_rows)], pair_box, 0)
+    first.wait_recv()
+    half_sum[...] = source[pl.ds(kept, half_rows), :] + pair_box[...]
+
+    def slot(k):
+        return pl.ds(pl.multiple_of((lax.rem(y, 2) * 16 + k) * rows, 8), rows)
+
+    def give(to_y, to_x, to_z, to_core, k):
+        at = pl.multiple_of((chip_of(to_y, to_x, to_z) - 32 * core) * rows, 8)
         pltpu.make_async_remote_copy(
-            src_ref=source.at[pl.ds(pl.multiple_of(index_in(group, to) * rows, 8), rows)],
-            dst_ref=box.at[pl.ds(k * rows, rows)],
-            send_sem=send.at[stage],
-            recv_sem=recv.at[stage],
-            device_id=device_of(to),
+            src_ref=half_sum.at[pl.ds(at, rows)],
+            dst_ref=box.at[slot(k)],
+            send_sem=sems.at[2],
+            recv_sem=sems.at[3],
+            device_id=device_of(to_y, to_x, to_z, to_core),
             device_id_type=MESH,
         ).start()
 
-
-def spread(near, out_ref, start, stage, rows, send, recv):
-    group = GROUPS[stage]
-    piece = out_ref.at[pl.ds(pl.multiple_of(start, 8), rows)]
-    for offsets in team(group):
+    def keep(to_y, to_x, to_z, to_core, k):
+        at = pl.multiple_of((here - 32 * core) * rows, 8)
+        box[slot(k), :] = half_sum[pl.ds(at, rows), :]
+
+    to_partners(near, give, keep)
+    meanwhile()
+    wait_partners(near, box, sems.at[3])
+    mine[...] = jnp.sum(box[...].reshape(32, rows, TILE), axis=0)
+    second = to_sibling(mine, twin, 2)
+    second.wait_recv()
+    total = mine[...] + twin[...]
+    second.wait_send()
+    mine[...] = total
+    place = pl.ds(pl.multiple_of(here * rows, 8), rows)
+
+    def spread(to_y, to_x, to_z, to_core, k):
         pltpu.make_async_remote_copy(
-            src_ref=piece,
-            dst_ref=piece,
-            send_sem=send.at[stage],
-            recv_sem=recv.at[stage],
-            device_id=device_of(member(near, group, offsets)),
+            src_ref=mine,
+            dst_ref=out_ref.at[place],
+            send_sem=sems.at[6],
+            recv_sem=sems.at[7],
+            device_id=device_of(to_y, to_x, to_z, to_core),
             device_id_type=MESH,
         ).start()
 
-
-def wait_bytes(box, sem):
-    pltpu.make_async_copy(box, box, sem).wait()
-
-
-def exchange(near, source, out_ref, works, boxes, send_in, recv_in, send_out, recv_out, meanwhile):
-    count = len(GROUPS)
-    start, starts = 0, []
-    for stage, group in enumerate(GROUPS):
-        size = size_of(group)
-        rows = source.shape[0] // size
-        box = boxes[stage]
-        scatter(near, source, stage, rows, box, send_in, recv_in)
-        me = pl.multiple_of(index_in(group, {axis: near[axis][0] for axis in SIZES}) * rows, 8)
-        if stage == count - 1:
-            meanwhile()
-        wait_bytes(box, recv_in.at[stage])
-        own = source[pl.ds(me, rows), :]
-        works[stage][...] = own + jnp.sum(box[...].reshape(size - 1, rows, TILE), axis=0)
-        start = start + me
-        starts.append(start)
-        source = works[stage]
-
-    out_ref[pl.ds(pl.multiple_of(start, 8), source.shape[0]), :] = source[...]
-    for stage in reversed(range(count)):
-        spread(near, out_ref, starts[stage], stage, works[stage].shape[0], send_out, recv_out)
-        wait_bytes(boxes[stage], recv_out.at[stage])
-    for stage in range(count):
-        wait_bytes(boxes[stage], send_in.at[stage])
-        wait_bytes(boxes[stage], send_out.at[stage])
+    def keep_sum(to_y, to_x, to_z, to_core, k):
+        out_ref[place, :] = total
+
+    to_partners(near, spread, keep_sum)
+    wait_partners(near, box, sems.at[7])
+    have = out_ref.at[pl.ds(kept, half_rows)]
+    third = to_sibling(have, have, 4)
+    third.wait_recv()
+    wait_partners(near, box, sems.at[2])
+    wait_partners(near, box, sems.at[6])
+    first.wait_send()
+    third.wait_send()
 
 
 def tile_kernel(
@@ -144,8 +187,7 @@
     out_ref, tran_ref, flip_ref, prec_ref, start_ref, tiles_ref, val_ref, wgt_ref, step_ref, block_ref, live_ref, lhs, info, curv, local, small_sem, tile_sem,
     *scratch,
 ):
-    count = len(GROUPS)
-    scratch, own = scratch[: 2 * count + 4], scratch[2 * count + 4 :]
+    scratch, own = scratch[:6], scratch[6:]
     tiles = op_ref.shape[0]
     each = tiles // PARTS
     small = ((live_hbm, live_ref), (wgt_hbm, wgt_ref), (val_hbm, val_ref), (step_hbm, step_ref), (block_hbm, block_ref),
@@ -211,7 +253,7 @@
     inform = (sums[:, :TILE] + sums[:, TILE : 2 * TILE]).reshape(segments // 8, 1, 8, TILE)
     observed = (sums[:, 2 * TILE : 3 * TILE] + sums[:, 3 * TILE :]).reshape(segments // 8, 1, 8, TILE)
     local[...] = jnp.concatenate([inform, observed], axis=1).reshape(2 * segments, TILE)
-    wait_all()
+    wait_all(near)
 
     def meanwhile():
         for copy in small[5:]:
@@ -221,7 +263,7 @@
                 a, b = slice(i * TILE, (i + 1) * TILE), slice(j * TILE, (j + 1) * TILE)
                 flip_ref[b, a] = jnp.transpose(tran_ref[a, b])
 
-    exchange(near, local, out_ref, scratch[:count], scratch[count : 2 * count], *scratch[2 * count :], meanwhile)
+    exchange(near, local, out_ref, *scratch, meanwhile)
     recurrence(out_ref, tran_ref, flip_ref, prec_ref, start_ref, filt_ref, smooth_ref, *own)
 
 
@@ -365,12 +407,6 @@
     tiles = op.shape[0]
     width = transition.shape[0]
     times = segments // 4
-    rows, works, boxes = 2 * segments, [], []
-    for group in GROUPS:
-        size = size_of(group)
-        rows //= size
-        works.append(pltpu.VMEM((rows, TILE), F32))
-        boxes.append(pltpu.VMEM(((size - 1) * rows, TILE), F32))
     hbm, vmem = pl.BlockSpec(memory_space=pltpu.HBM), pl.BlockSpec(memory_space=pltpu.VMEM)
     shape = jax.ShapeDtypeStruct((4, width), F32)
     return pl.pallas_call(
@@ -396,9 +432,12 @@
             pltpu.VMEM((2 * segments, TILE), F32),
             pltpu.SemaphoreType.DMA((8,)),
             pltpu.SemaphoreType.DMA((PARTS,)),
-            *works,
-            *boxes,
-            *[pltpu.SemaphoreType.DMA((len(GROUPS),))] * 4,
+            pltpu.VMEM((segments, TILE), F32),
+            pltpu.VMEM((segments, TILE), F32),
+            pltpu.VMEM((segments, TILE), F32),
+            pltpu.VMEM((segments // 32, TILE), F32),
+            pltpu.VMEM((segments // 32, TILE), F32),
+            pltpu.SemaphoreType.DMA((10,)),
             pltpu.VMEM((segments, TILE), F32),
             pltpu.VMEM((segments, TILE), F32),
             pltpu.VMEM((4, times // 2, TILE), F32),

time: 60.4 us -> 62.4 us (1.033)
  Pallas kernels: 56.9 us -> 58.9 us
    pallas_call x1, Pallas kernels: 56.9 us -> 58.9 us  [smoother(): pl.pallas_call(tile_kernel, out_shape=(shape, shape), in_specs=[hbm] * 9,...]
where the time goes in v4:
time: 62.4 us; the launch traced here: 62.1 us
  Pallas kernels  58.9 us (94%)
  local copies, waits for them, and re-layouts  2.59 us (4%)
  between operations  0.64 us (1%)
    pallas_call x1, Pallas kernels, smoother(): pl.pallas_call(tile_kernel, out_shape=(shape, shape), in_specs=[hbm] * 9,...  58.9 us
    unnamed x2, local copies, waits for them, and re-layouts  2.59 us

profile of v4, /device:TPU:1, one launch (start us, length us, event | category | flops | bytes accessed | tf_op | source)
XLA Modules:
  0.0 62.1 jit_solution(16484491993439688728)
XLA Ops:
  0.6 58.9 %shard_map.104 = (f32[4,512]{1,0:T(4,128)}, f32[4,512]{1,0:T(4,128)}) custom-call(bf16[256,128,128]{2,1,0:T(8,128)(2,1)} %op_ref.1, bf16[256,128]{1,0:T(8,128)(2,1)} %val_hbm.1, f32[256,128]{1,0:T(8,128)} %wgt_hbm.1, s32[1,256]{1,0:T(1,128)} %bitcast.7, s32[1,256]{1,0:T(1,128)} %bitcast.8, s32[1,256]{1,0:T(1,128)} %bitcast.9, f32[512,512]{1,0:T(8,128)} %tran_hbm.1, ...), custom_call_target="tpu_custom_call" | custom-call | tf_op jit(solution)/shard_map/pallas_call | solution.py:412
  59.5 1.3 %copy.13 = f32[4,512]{1,0:T(4,128)} copy(f32[4,512]{1,0:T(4,128)} %get-tuple-element.4) | data formatting | bytes 16384
  60.8 1.3 %copy.14 = f32[4,512]{1,0:T(4,128)} copy(f32[4,512]{1,0:T(4,128)} %get-tuple-element.5) | data formatting | bytes 16384

commit v5 on v3

--- a/solution.py
+++ b/solution.py
@@ -140,7 +140,7 @@
 
 def tile_kernel(
     op_ref, val_hbm, wgt_hbm, step_hbm, block_hbm, live_hbm, tran_hbm, prec_hbm, start_hbm,
-    filt_ref, smooth_ref,
+    both_ref,
     out_ref, tran_ref, flip_ref, prec_ref, start_ref, tiles_ref, val_ref, wgt_ref, step_ref, block_ref, live_ref, lhs, info, curv, local, small_sem, tile_sem,
     *scratch,
 ):
@@ -222,11 +222,11 @@
                 flip_ref[b, a] = jnp.transpose(tran_ref[a, b])
 
     exchange(near, local, out_ref, scratch[:count], scratch[count : 2 * count], *scratch[2 * count :], meanwhile)
-    recurrence(out_ref, tran_ref, flip_ref, prec_ref, start_ref, filt_ref, smooth_ref, *own)
+    recurrence(out_ref, tran_ref, flip_ref, prec_ref, start_ref, both_ref, *own)
 
 
 def recurrence(
-    sums_ref, tran_ref, flip_ref, prec_ref, start_ref, filt_ref, smooth_ref,
+    sums_ref, tran_ref, flip_ref, prec_ref, start_ref, both_ref,
     gain, drive, drive_on, drive_back, gain_col, diff_col, diff_row, filt_row, extra_row, filt_col, extra_col,
 ):
     segments = sums_ref.shape[0] // 2
@@ -243,11 +243,18 @@
     inverse = 1.0 / (pp + observed)
     gain[...] = (pp * inverse).reshape(segments, TILE)
     drive[...] = (inform * inverse).reshape(segments, TILE)
-    for b in range(4):
-        rows = slice(b * TILE, (b + 1) * TILE)
-        g = jnp.transpose(gain[pl.ds(b, times, 4), :])
-        for i in range(half):
-            gain_col[i, rows, :] = jnp.broadcast_to(g[:, 2 * i : 2 * i + 1], (TILE, TILE))
+    even_gain = jnp.concatenate([gain[pl.ds(b, half, 8), :] for b in range(4)], axis=1)
+    upper = even_gain.astype(BF16).astype(F32)
+    stack = jnp.concatenate([upper, even_gain - upper], axis=0)
+    turned = [jnp.transpose(stack[:, b * TILE : (b + 1) * TILE]) for b in range(4)]
+    turned = jnp.concatenate(turned, axis=0).astype(BF16)
+    lane = lax.rem(lax.broadcasted_iota(jnp.int32, (TILE, 2 * TILE), 0), half)
+    pair = lax.div(lax.broadcasted_iota(jnp.int32, (TILE, 2 * TILE), 1), TILE)
+    for n in range(half // 2):
+        pick = jnp.where(lane == 2 * n + pair, 1.0, 0.0).astype(BF16)
+        wide = jnp.dot(turned, pick, preferred_element_type=F32)
+        gain_col[2 * n] = wide[:, :TILE]
+        gain_col[2 * n + 1] = wide[:, TILE:]
 
     even_drive = jnp.concatenate([drive[pl.ds(b, half, 8), :] for b in range(4)], axis=1)
     upper, lower = parts(even_drive)
@@ -353,12 +360,12 @@
             f = jnp.sum(jnp.where(eye, filt_col[keep, lane, :], 0.0), axis=0, keepdims=True)
             f = f + drive[pl.ds(8 * (first + keep) + b, 1), :]
             e = jnp.sum(jnp.where(eye, extra_col[keep, lane, :], 0.0), axis=0, keepdims=True)
-            filt_ref[2 * keep : 2 * keep + 1, lane] = f
-            smooth_ref[2 * keep : 2 * keep + 1, lane] = f + e
+            both_ref[2 * keep : 2 * keep + 1, lane] = f
+            both_ref[4 + 2 * keep : 5 + 2 * keep, lane] = e
             at = pl.ds(4 * (2 * (first + keep) + 1) + b, 1)
             f = filt_row[at, :]
-            filt_ref[2 * keep + 1 : 2 * keep + 2, lane] = f
-            smooth_ref[2 * keep + 1 : 2 * keep + 2, lane] = f + extra_row[at, :]
+            both_ref[2 * keep + 1 : 2 * keep + 2, lane] = f
+            both_ref[5 + 2 * keep : 6 + 2 * keep, lane] = extra_row[at, :]
 
 
 def smoother(op, val, wgt, step, block, live, transition, predicted_precision, starting_mean, segments):
@@ -372,12 +379,11 @@
         works.append(pltpu.VMEM((rows, TILE), F32))
         boxes.append(pltpu.VMEM(((size - 1) * rows, TILE), F32))
     hbm, vmem = pl.BlockSpec(memory_space=pltpu.HBM), pl.BlockSpec(memory_space=pltpu.VMEM)
-    shape = jax.ShapeDtypeStruct((4, width), F32)
-    return pl.pallas_call(
+    both = pl.pallas_call(
         tile_kernel,
-        out_shape=(shape, shape),
+        out_shape=jax.ShapeDtypeStruct((8, width), F32),
         in_specs=[hbm] * 9,
-        out_specs=(vmem, vmem),
+        out_specs=vmem,
         scratch_shapes=[
             pltpu.VMEM((2 * segments, TILE), F32),
             pltpu.VMEM((width, width), F32),
@@ -425,6 +431,7 @@
         predicted_precision.reshape(4, TILE),
         starting_mean.reshape(4, TILE),
     )
+    return both[:4], both[:4] + both[4:]
 
 
 def shards(op, val, wgt, step, block, live, transition, predicted_precision, starting_mean):

time: 60.4 us -> 57 us (0.944)
  local copies, waits for them, and re-layouts: 2.59 us -> 0 us
  Pallas kernels: 56.9 us -> 54.8 us
  other arithmetic: 0 us -> 1.4 us
    unnamed x2 -> x0, local copies, waits for them, and re-layouts: 2.59 us -> none
    pallas_call x1, Pallas kernels: 56.9 us -> 54.8 us  [smoother(): pl.pallas_call(tile_kernel, out_shape=jax.ShapeDtypeStruct((8, width), F3...]
    add x0 -> x1, other arithmetic: none -> 1.4 us  [smoother(): return (both[:4], both[:4] + both[4:])]
where the time goes in v5:
time: 57 us; the launch traced here: 56.8 us
  Pallas kernels  54.8 us (96%)
  other arithmetic  1.4 us (2%)
  between operations  0.64 us (1%)
    pallas_call x1, Pallas kernels, smoother(): pl.pallas_call(tile_kernel, out_shape=jax.ShapeDtypeStruct((8, width), F3...  54.8 us
    add x1, other arithmetic, smoother(): return (both[:4], both[:4] + both[4:])  1.4 us

profile of v5, /device:TPU:1, one launch (start us, length us, event | category | flops | bytes accessed | tf_op | source)
XLA Modules:
  0.0 56.8 jit_solution(7043714549136689582)
XLA Ops:
  0.6 54.8 %shard_map.104 = f32[8,512]{1,0:T(8,128)} custom-call(bf16[256,128,128]{2,1,0:T(8,128)(2,1)} %op_ref.1, bf16[256,128]{1,0:T(8,128)(2,1)} %val_hbm.1, f32[256,128]{1,0:T(8,128)} %wgt_hbm.1, s32[1,256]{1,0:T(1,128)} %bitcast.7, s32[1,256]{1,0:T(1,128)} %bitcast.8, s32[1,256]{1,0:T(1,128)} %bitcast.9, f32[512,512]{1,0:T(8,128)} %tran_hbm.1, f32[4,128]{1,0:T(4,128)} %bitcast.5, ...), custom_call_target="tpu_custom_call" | custom-call | tf_op jit(solution)/shard_map/pallas_call | solution.py:382
  55.4 1.4 %slice_add_fusion = (f32[4,512]{1,0:T(4,128)}, f32[4,512]{1,0:T(4,128)}) fusion(f32[8,512]{1,0:T(8,128)} %shard_map.104), kind=kLoop, calls=%fused_computation | loop fusion | flops 2048 | bytes 32768 | tf_op jit(solution)/shard_map/add | solution.py:434

commit v6 on v5

--- a/solution.py
+++ b/solution.py
@@ -13,7 +13,7 @@
 GROUPS = (("c",), ("y", "x", "z"))
 SIZES = {"c": 2, "x": 4, "y": 4, "z": 4}
 CHUNK = 128
-PARTS = 8
+PARTS = 4
 F32, BF16 = jnp.float32, jnp.bfloat16
 
 
@@ -132,10 +132,16 @@
     out_ref[pl.ds(pl.multiple_of(start, 8), source.shape[0]), :] = source[...]
     for stage in reversed(range(count)):
         spread(near, out_ref, starts[stage], stage, works[stage].shape[0], send_out, recv_out)
-        wait_bytes(boxes[stage], recv_out.at[stage])
-    for stage in range(count):
-        wait_bytes(boxes[stage], send_in.at[stage])
-        wait_bytes(boxes[stage], send_out.at[stage])
+        if stage > 0:
+            wait_bytes(boxes[stage], recv_out.at[stage])
+
+    def arrived():
+        wait_bytes(boxes[0], recv_out.at[0])
+        for stage in range(count):
+            wait_bytes(boxes[stage], send_in.at[stage])
+            wait_bytes(boxes[stage], send_out.at[stage])
+
+    return arrived
 
 
 def tile_kernel(
@@ -221,12 +227,12 @@
                 a, b = slice(i * TILE, (i + 1) * TILE), slice(j * TILE, (j + 1) * TILE)
                 flip_ref[b, a] = jnp.transpose(tran_ref[a, b])
 
-    exchange(near, local, out_ref, scratch[:count], scratch[count : 2 * count], *scratch[2 * count :], meanwhile)
-    recurrence(out_ref, tran_ref, flip_ref, prec_ref, start_ref, both_ref, *own)
+    arrived = exchange(near, local, out_ref, scratch[:count], scratch[count : 2 * count], *scratch[2 * count :], meanwhile)
+    recurrence(arrived, own[0], out_ref, tran_ref, flip_ref, prec_ref, start_ref, both_ref, *own[1:])
 
 
 def recurrence(
-    sums_ref, tran_ref, flip_ref, prec_ref, start_ref, both_ref,
+    arrived, part_gain, sums_ref, tran_ref, flip_ref, prec_ref, start_ref, both_ref,
     gain, drive, drive_on, drive_back, gain_col, diff_col, diff_row, filt_row, extra_row, filt_col, extra_col,
 ):
     segments = sums_ref.shape[0] // 2
@@ -238,23 +244,33 @@
 
     pp = prec_ref[...]
     pp = jnp.concatenate([pp, pp], axis=0)[None]
-    both = sums_ref[...].reshape(segments // 8, 2, 8, TILE)
-    inform, observed = both[:, 0], both[:, 1]
-    inverse = 1.0 / (pp + observed)
-    gain[...] = (pp * inverse).reshape(segments, TILE)
-    drive[...] = (inform * inverse).reshape(segments, TILE)
-    even_gain = jnp.concatenate([gain[pl.ds(b, half, 8), :] for b in range(4)], axis=1)
-    upper = even_gain.astype(BF16).astype(F32)
-    stack = jnp.concatenate([upper, even_gain - upper], axis=0)
-    turned = [jnp.transpose(stack[:, b * TILE : (b + 1) * TILE]) for b in range(4)]
-    turned = jnp.concatenate(turned, axis=0).astype(BF16)
-    lane = lax.rem(lax.broadcasted_iota(jnp.int32, (TILE, 2 * TILE), 0), half)
-    pair = lax.div(lax.broadcasted_iota(jnp.int32, (TILE, 2 * TILE), 1), TILE)
-    for n in range(half // 2):
-        pick = jnp.where(lane == 2 * n + pair, 1.0, 0.0).astype(BF16)
-        wide = jnp.dot(turned, pick, preferred_element_type=F32)
-        gain_col[2 * n] = wide[:, :TILE]
-        gain_col[2 * n + 1] = wide[:, TILE:]
+    lane = lax.rem(lax.broadcasted_iota(jnp.int32, (half, 2 * TILE), 0), half // 2)
+    pair = lax.div(lax.broadcasted_iota(jnp.int32, (half, 2 * TILE), 1), TILE)
+
+    def prepare(part):
+        rows = segments // 2
+        both = sums_ref[pl.ds(pl.multiple_of(part * segments, 8), segments), :].reshape(rows // 8, 2, 8, TILE)
+        inverse = 1.0 / (pp + both[:, 1])
+        value = (pp * inverse).reshape(rows, TILE)
+        here = pl.ds(pl.multiple_of(part * rows, 8), rows)
+        gain[here, :] = value
+        drive[here, :] = (both[:, 0] * inverse).reshape(rows, TILE)
+        part_gain[...] = value
+        even_gain = jnp.concatenate([part_gain[pl.ds(b, half // 2, 8), :] for b in range(4)], axis=1)
+        upper = even_gain.astype(BF16).astype(F32)
+        stack = jnp.concatenate([upper, even_gain - upper], axis=0)
+        turned = [jnp.transpose(stack[:, b * TILE : (b + 1) * TILE]) for b in range(4)]
+        turned = jnp.concatenate(turned, axis=0).astype(BF16)
+        for n in range(half // 4):
+            pick = jnp.where(lane == 2 * n + pair, 1.0, 0.0).astype(BF16)
+            wide = jnp.dot(turned, pick, preferred_element_type=F32)
+            gain_col[part * (half // 2) + 2 * n] = wide[:, :TILE]
+            gain_col[part * (half // 2) + 2 * n + 1] = wide[:, TILE:]
+
+    core = lax.rem(lax.axis_index("tm"), 2)
+    prepare(core)
+    arrived()
+    prepare(1 - core)
 
     even_drive = jnp.concatenate([drive[pl.ds(b, half, 8), :] for b in range(4)], axis=1)
     upper, lower = parts(even_drive)
@@ -405,6 +421,7 @@
             *works,
             *boxes,
             *[pltpu.SemaphoreType.DMA((len(GROUPS),))] * 4,
+            pltpu.VMEM((segments // 2, TILE), F32),
             pltpu.VMEM((segments, TILE), F32),
             pltpu.VMEM((segments, TILE), F32),
             pltpu.VMEM((4, times // 2, TILE), F32),

time: 57 us -> 55.6 us (0.975)
  Pallas kernels: 54.8 us -> 53.4 us
    pallas_call x1, Pallas kernels: 54.8 us -> 53.4 us  [smoother(): pl.pallas_call(tile_kernel, out_shape=jax.ShapeDtypeStruct((8, width), F3...]
where the time goes in v6:
time: 55.6 us; the launch traced here: 55.5 us
  Pallas kernels  53.4 us (96%)
  other arithmetic  1.4 us (3%)
  between operations  0.64 us (1%)
    pallas_call x1, Pallas kernels, smoother(): pl.pallas_call(tile_kernel, out_shape=jax.ShapeDtypeStruct((8, width), F3...  53.4 us
    add x1, other arithmetic, smoother(): return (both[:4], both[:4] + both[4:])  1.4 us

profile of v6, /device:TPU:1, one launch (start us, length us, event | category | flops | bytes accessed | tf_op | source)
XLA Modules:
  0.0 55.5 jit_solution(5620565935262033702)
XLA Ops:
  0.6 53.4 %shard_map.104 = f32[8,512]{1,0:T(8,128)} custom-call(bf16[256,128,128]{2,1,0:T(8,128)(2,1)} %op_ref.1, bf16[256,128]{1,0:T(8,128)(2,1)} %val_hbm.1, f32[256,128]{1,0:T(8,128)} %wgt_hbm.1, s32[1,256]{1,0:T(1,128)} %bitcast.7, s32[1,256]{1,0:T(1,128)} %bitcast.8, s32[1,256]{1,0:T(1,128)} %bitcast.9, f32[512,512]{1,0:T(8,128)} %tran_hbm.1, f32[4,128]{1,0:T(4,128)} %bitcast.5, ...), custom_call_target="tpu_custom_call" | custom-call | tf_op jit(solution)/shard_map/pallas_call | solution.py:398
  54.1 1.4 %slice_add_fusion = (f32[4,512]{1,0:T(4,128)}, f32[4,512]{1,0:T(4,128)}) fusion(f32[8,512]{1,0:T(8,128)} %shard_map.104), kind=kLoop, calls=%fused_computation | loop fusion | flops 2048 | bytes 32768 | tf_op jit(solution)/shard_map/add | solution.py:451

commit v7 on v6

--- a/solution.py
+++ b/solution.py
@@ -79,20 +79,6 @@
     pl.semaphore_wait(pltpu.get_barrier_semaphore(), sum(size_of(group) - 1 for group in GROUPS))
 
 
-def scatter(near, source, stage, rows, box, send, recv):
-    group = GROUPS[stage]
-    for k, offsets in enumerate(team(group)):
-        to = member(near, group, offsets)
-        pltpu.make_async_remote_copy(
-            src_ref=source.at[pl.ds(pl.multiple_of(index_in(group, to) * rows, 8), rows)],
-            dst_ref=box.at[pl.ds(k * rows, rows)],
-            send_sem=send.at[stage],
-            recv_sem=recv.at[stage],
-            device_id=device_of(to),
-            device_id_type=MESH,
-        ).start()
-
-
 def spread(near, out_ref, start, stage, rows, send, recv):
     group = GROUPS[stage]
     piece = out_ref.at[pl.ds(pl.multiple_of(start, 8), rows)]
@@ -111,23 +97,51 @@
     pltpu.make_async_copy(box, box, sem).wait()
 
 
-def exchange(near, source, out_ref, works, boxes, send_in, recv_in, send_out, recv_out, meanwhile):
+def exchange(near, source, out_ref, works, boxes, pair_send, pair_recv, send_in, recv_in, send_out, recv_out, meanwhile):
     count = len(GROUPS)
-    start, starts = 0, []
-    for stage, group in enumerate(GROUPS):
-        size = size_of(group)
-        rows = source.shape[0] // size
-        box = boxes[stage]
-        scatter(near, source, stage, rows, box, send_in, recv_in)
-        me = pl.multiple_of(index_in(group, {axis: near[axis][0] for axis in SIZES}) * rows, 8)
-        if stage == count - 1:
-            meanwhile()
-        wait_bytes(box, recv_in.at[stage])
-        own = source[pl.ds(me, rows), :]
-        works[stage][...] = own + jnp.sum(box[...].reshape(size - 1, rows, TILE), axis=0)
-        start = start + me
-        starts.append(start)
-        source = works[stage]
+    mine = {axis: near[axis][0] for axis in SIZES}
+    half_rows, piece_rows = works[0].shape[0], works[1].shape[0]
+    block = half_rows // SIZES["y"]
+    order = (2, 1, 3, 0)
+    halves = [near["c"][k] * half_rows for k in range(2)]
+    sibling = device_of(member(near, ("c",), (1,)))
+
+    def block_at(base, offset):
+        return pl.ds(pl.multiple_of(base + near["y"][offset] * block, 8), block)
+
+    for k, offset in enumerate(order):
+        pltpu.make_async_remote_copy(
+            src_ref=source.at[block_at(halves[1], offset)],
+            dst_ref=boxes[0].at[block_at(0, offset)],
+            send_sem=pair_send.at[k],
+            recv_sem=pair_recv.at[k],
+            device_id=sibling,
+            device_id_type=MESH,
+        ).start()
+    everyone = team(GROUPS[1])
+    for k, offset in enumerate(order):
+        here = block_at(0, offset)
+        wait_bytes(boxes[0].at[here], pair_recv.at[k])
+        works[0][here, :] = source[block_at(halves[0], offset), :] + boxes[0][here, :]
+        for slot, offsets in enumerate(everyone):
+            if offsets[0] == offset:
+                to = member(near, GROUPS[1], offsets)
+                at = pl.multiple_of(index_in(GROUPS[1], to) * piece_rows, 8)
+                pltpu.make_async_remote_copy(
+                    src_ref=works[0].at[pl.ds(at, piece_rows)],
+                    dst_ref=boxes[1].at[pl.ds(slot * piece_rows, piece_rows)],
+                    send_sem=send_in.at[1],
+                    recv_sem=recv_in.at[1],
+                    device_id=device_of(to),
+                    device_id_type=MESH,
+                ).start()
+    meanwhile()
+    wait_bytes(boxes[1], recv_in.at[1])
+    me = index_in(GROUPS[1], mine) * piece_rows
+    own = works[0][pl.ds(pl.multiple_of(me, 8), piece_rows), :]
+    works[1][...] = own + jnp.sum(boxes[1][...].reshape(len(everyone), piece_rows, TILE), axis=0)
+    starts = [halves[0], halves[0] + me]
+    start, source = starts[1], works[1]
 
     out_ref[pl.ds(pl.multiple_of(start, 8), source.shape[0]), :] = source[...]
     for stage in reversed(range(count)):
@@ -137,8 +151,10 @@
 
     def arrived():
         wait_bytes(boxes[0], recv_out.at[0])
+        for k in range(SIZES["y"]):
+            wait_bytes(boxes[0].at[pl.ds(0, block)], pair_send.at[k])
+        wait_bytes(boxes[1], send_in.at[1])
         for stage in range(count):
-            wait_bytes(boxes[stage], send_in.at[stage])
             wait_bytes(boxes[stage], send_out.at[stage])
 
     return arrived
@@ -151,7 +167,7 @@
     *scratch,
 ):
     count = len(GROUPS)
-    scratch, own = scratch[: 2 * count + 4], scratch[2 * count + 4 :]
+    scratch, own = scratch[: 2 * count + 6], scratch[2 * count + 6 :]
     tiles = op_ref.shape[0]
     each = tiles // PARTS
     small = ((live_hbm, live_ref), (wgt_hbm, wgt_ref), (val_hbm, val_ref), (step_hbm, step_ref), (block_hbm, block_ref),
@@ -420,6 +436,7 @@
             pltpu.SemaphoreType.DMA((PARTS,)),
             *works,
             *boxes,
+            *[pltpu.SemaphoreType.DMA((SIZES["y"],))] * 2,
             *[pltpu.SemaphoreType.DMA((len(GROUPS),))] * 4,
             pltpu.VMEM((segments // 2, TILE), F32),
             pltpu.VMEM((segments, TILE), F32),

time: 55.6 us -> 55.3 us (level)
  no operation moved by 1% of the time
where the time goes in v7:
time: 55.3 us; the launch traced here: 55.1 us
  Pallas kernels  53.1 us (96%)
  other arithmetic  1.4 us (3%)
  between operations  0.64 us (1%)
    pallas_call x1, Pallas kernels, smoother(): pl.pallas_call(tile_kernel, out_shape=jax.ShapeDtypeStruct((8, width), F3...  53.1 us
    add x1, other arithmetic, smoother(): return (both[:4], both[:4] + both[4:])  1.4 us

profile of v7, /device:TPU:1, one launch (start us, length us, event | category | flops | bytes accessed | tf_op | source)
XLA Modules:
  0.0 55.1 jit_solution(16524636435467733887)
XLA Ops:
  0.6 53.1 %shard_map.104 = f32[8,512]{1,0:T(8,128)} custom-call(bf16[256,128,128]{2,1,0:T(8,128)(2,1)} %op_ref.1, bf16[256,128]{1,0:T(8,128)(2,1)} %val_hbm.1, f32[256,128]{1,0:T(8,128)} %wgt_hbm.1, s32[1,256]{1,0:T(1,128)} %bitcast.7, s32[1,256]{1,0:T(1,128)} %bitcast.8, s32[1,256]{1,0:T(1,128)} %bitcast.9, f32[512,512]{1,0:T(8,128)} %tran_hbm.1, f32[4,128]{1,0:T(4,128)} %bitcast.5, ...), custom_call_target="tpu_custom_call" | custom-call | tf_op jit(solution)/shard_map/pallas_call | solution.py:414
  53.7 1.4 %slice_add_fusion = (f32[4,512]{1,0:T(4,128)}, f32[4,512]{1,0:T(4,128)}) fusion(f32[8,512]{1,0:T(8,128)} %shard_map.104), kind=kLoop, calls=%fused_computation | loop fusion | flops 2048 | bytes 32768 | tf_op jit(solution)/shard_map/add | solution.py:468

commit v8 on v7

--- a/solution.py
+++ b/solution.py
@@ -12,7 +12,9 @@
 TILE = 128
 GROUPS = (("c",), ("y", "x", "z"))
 SIZES = {"c": 2, "x": 4, "y": 4, "z": 4}
-CHUNK = 128
+CHUNK = 32
+DEPTH = 2
+ACCS = 1
 PARTS = 4
 F32, BF16 = jnp.float32, jnp.bfloat16
 
@@ -311,8 +313,14 @@
         return jnp.sum(total, axis=2, keepdims=True)
 
     def gather(ref, col, c, sums):
-        for b in range(4):
-            sums[b].append(jnp.sum(block(ref, c, b) * col, axis=0))
+        for k in range(CHUNK // 8):
+            for b in range(4):
+                term = ref[c * CHUNK + 8 * k : c * CHUNK + 8 * k + 8, b * TILE : (b + 1) * TILE] * col[k]
+                slot = k % ACCS
+                if c == 0 and k < ACCS:
+                    sums[b].append(term)
+                else:
+                    sums[b][slot] = sums[b][slot] + term
 
     def finish(pieces):
         while len(pieces) > 1:
@@ -326,14 +334,21 @@
         even, odd = 2 * i, 2 * i + 1
         wide = spread(row)
         sums = [[] for _ in range(4)]
-        for c in range(chunks):
+        def use(c, bare):
             rows = slice(c * CHUNK, (c + 1) * CHUNK)
-            bare = row_to_col(tran_ref, wide, c)
             col = part(gain_col, c, i) * bare
             gather(flip_ref, col, c, sums)
             diff_col[i, rows, :] = (col - bare).reshape(CHUNK, TILE)
             if keep is not None:
                 filt_col[keep, rows, :] = col.reshape(CHUNK, TILE)
+
+        pending = []
+        for c in range(chunks):
+            pending.append((c, row_to_col(tran_ref, wide, c)))
+            if len(pending) > DEPTH:
+                use(*pending.pop(0))
+        for item in pending:
+            use(*item)
         out = []
         for b in range(4):
             at = pl.ds(4 * odd + b, 1)
@@ -370,12 +385,20 @@
     def backward(keep, i, row):
         wide = spread(row)
         sums = [[] for _ in range(4)]
-        for c in range(chunks):
-            col = part(gain_col, c, i) * row_to_col(flip_ref, wide, c)
+        def use(c, bare):
+            col = part(gain_col, c, i) * bare
             if keep is not None:
                 extra_col[keep, c * CHUNK : (c + 1) * CHUNK, :] = col.reshape(CHUNK, TILE)
             if keep != 0:
                 gather(tran_ref, col + part(diff_col, c, i), c, sums)
+
+        pending = []
+        for c in range(chunks):
+            pending.append((c, row_to_col(flip_ref, wide, c)))
+            if len(pending) > DEPTH:
+                use(*pending.pop(0))
+        for item in pending:
+            use(*item)
         if keep == 0:
             return row
         moved = [drive_back[b, pl.ds(i, 1), :] for b in range(4)]

time: 55.3 us -> 55 us (level)
  no operation moved by 1% of the time
where the time goes in v8:
time: 55 us; the launch traced here: 54.8 us
  Pallas kernels  52.8 us (96%)
  other arithmetic  1.4 us (3%)
  between operations  0.64 us (1%)
    pallas_call x1, Pallas kernels, smoother(): pl.pallas_call(tile_kernel, out_shape=jax.ShapeDtypeStruct((8, width), F3...  52.8 us
    add x1, other arithmetic, smoother(): return (both[:4], both[:4] + both[4:])  1.4 us

profile of v8, /device:TPU:1, one launch (start us, length us, event | category | flops | bytes accessed | tf_op | source)
XLA Modules:
  0.0 54.8 jit_solution(417349506819241537)
XLA Ops:
  0.6 52.8 %shard_map.104 = f32[8,512]{1,0:T(8,128)} custom-call(bf16[256,128,128]{2,1,0:T(8,128)(2,1)} %op_ref.1, bf16[256,128]{1,0:T(8,128)(2,1)} %val_hbm.1, f32[256,128]{1,0:T(8,128)} %wgt_hbm.1, s32[1,256]{1,0:T(1,128)} %bitcast.7, s32[1,256]{1,0:T(1,128)} %bitcast.8, s32[1,256]{1,0:T(1,128)} %bitcast.9, f32[512,512]{1,0:T(8,128)} %tran_hbm.1, f32[4,128]{1,0:T(4,128)} %bitcast.5, ...), custom_call_target="tpu_custom_call" | custom-call | tf_op jit(solution)/shard_map/pallas_call | solution.py:437
  53.4 1.4 %slice_add_fusion = (f32[4,512]{1,0:T(4,128)}, f32[4,512]{1,0:T(4,128)}) fusion(f32[8,512]{1,0:T(8,128)} %shard_map.104), kind=kLoop, calls=%fused_computation | loop fusion | flops 2048 | bytes 32768 | tf_op jit(solution)/shard_map/add | solution.py:491
